TPU v7x, 128 devices: a whole 4x4x4 slice. The times are simulated.
128 devices in a mesh: grp: 16 (over y, x), sp: 8 (over z, core).
Axes of the slice: x: 4, y: 4, z: 4, core: 2. Of those that a mesh axis runs over, the one named last changes fastest.
Arguments:
- clips: bfloat16 [32, 8, 256, 1152], P('grp', None, 'sp'), may hold values from -6 to 6
- counts: int32 [32], replicated, may hold values from 2 to 8, as said below
- dest: int32 [16], replicated, may hold values from 0 to 15, each once
- weight_qkv: bfloat16 [1152, 3456], replicated, may hold values from -0.1875 to 0.1875
- weight_out: bfloat16 [1152, 1152], replicated, may hold values from -0.1875 to 0.1875
- cotangent: bfloat16 [32, 8, 256, 1152], P('grp', None, 'sp'), may hold values from -6 to 6
Outputs:
- outputs: bfloat16 [32, 8, 256, 1152], P('grp', None, 'sp')
- grad_clips: bfloat16 [32, 8, 256, 1152], P('grp', None, 'sp')
Inputs may be any that keep to these rules, and one draw needn't show every extreme that they name: `counts`: every clip uses 2 to 8 frames; some clip uses 8 and some uses 2.
All inputs are finite; a program needn't handle non-finite values.
Results may differ from a plain program's by a relative error of at most 0.0065.
Values may be sent and summed in bfloat16 or wider, within the bound.
No kernel may reach another device: no remote copies, remote signals or barrier semaphores. Data moves between devices by JAX's collectives and lax.ppermute only.
A program may use at most 128 MiB of HBM per device.

v0:
```python
import jax
import jax.numpy as jnp
from jax import lax
from jax.sharding import PartitionSpec as P

HEADS = 16


def normed_fn(values):
    mean = jnp.mean(values, axis=-1, keepdims=True)
    centered = values - mean
    var = jnp.mean(centered * centered, axis=-1, keepdims=True)
    return centered * lax.rsqrt(var + 1e-06)


def attend(query, keys, values):
    scale = query.shape[-1] ** (-0.5)
    scores = (
        jnp.einsum("...qhe,...khe->...hqk", query, keys, preferred_element_type=jnp.float32) * scale
    )
    scores = scores - jnp.max(scores, axis=-1, keepdims=True)
    weights = jnp.exp(scores)
    probs = (weights / jnp.sum(weights, axis=-1, keepdims=True)).astype(jnp.bfloat16)
    return jnp.einsum("...hqk,...khe->...qhe", probs, values, preferred_element_type=jnp.float32)


def on_device(clips, counts, dest, weight_qkv, weight_out, cotangent):
    groups = lax.axis_size("grp")
    me_group = lax.axis_index("grp")
    order = jnp.arange(groups, dtype=jnp.int32)
    source = jnp.sum(jnp.where(dest == me_group, order, 0))
    target = dest[me_group]
    outbox = clips[1:2]
    sending = jnp.where((order == target)[:, None, None, None], outbox, jnp.zeros_like(outbox))
    received = lax.all_to_all(sending, "grp", split_axis=0, concat_axis=0, tiled=True)
    arrived = lax.dynamic_slice_in_dim(received, source, 1, 0)
    work = jnp.concatenate([clips[0:1], arrived], axis=0)
    used = jnp.stack([counts[2 * me_group], counts[2 * source + 1]])
    frames = work.shape[1]
    width = work.shape[-1]
    head_dim = width // HEADS
    keep = (jnp.arange(frames, dtype=jnp.int32)[None, :] < used[:, None])[:, :, None, None]
    work_f = work.astype(jnp.float32)
    normed, norm_back = jax.vjp(normed_fn, work_f)
    qkv = jnp.dot(
        normed.astype(jnp.bfloat16), weight_qkv, preferred_element_type=jnp.float32
    ).astype(jnp.bfloat16)
    qkv = qkv.reshape(work.shape[:-1] + (3, HEADS, head_dim))
    qkv_heads = lax.all_to_all(qkv, "sp", split_axis=4, concat_axis=2, tiled=True)
    attended, attend_back = jax.vjp(
        attend, qkv_heads[..., 0, :, :], qkv_heads[..., 1, :, :], qkv_heads[..., 2, :, :]
    )
    attended = lax.all_to_all(
        attended.astype(jnp.bfloat16), "sp", split_axis=2, concat_axis=3, tiled=True
    )
    projected = jnp.dot(
        attended.reshape(work.shape), weight_out, preferred_element_type=jnp.float32
    )
    outputs = jnp.where(keep, work_f + projected, 0.0).astype(jnp.bfloat16)
    grad_out = jnp.where(keep, cotangent, jnp.zeros_like(cotangent))
    grad_att = jnp.einsum(
        "cfsd,ed->cfse", grad_out, weight_out, preferred_element_type=jnp.float32
    ).astype(jnp.bfloat16)
    grad_att = grad_att.reshape(work.shape[:-1] + (HEADS, head_dim))
    grad_att = lax.all_to_all(grad_att, "sp", split_axis=3, concat_axis=2, tiled=True)
    grad_q, grad_k, grad_v = attend_back(grad_att.astype(jnp.float32))
    grad_qkv = jnp.stack([grad_q, grad_k, grad_v], axis=-3)
    grad_qkv = lax.all_to_all(grad_qkv, "sp", split_axis=2, concat_axis=4, tiled=True)
    grad_qkv = grad_qkv.reshape(work.shape[:-1] + (3 * width,))
    grad_norm = jnp.einsum(
        "cfse,de->cfsd", grad_qkv, weight_qkv, preferred_element_type=jnp.float32
    )
    grad_work = (grad_out.astype(jnp.float32) + norm_back(grad_norm)[0]).astype(jnp.bfloat16)
    handed = grad_work[1:2]
    sending_back = jnp.where((order == source)[:, None, None, None], handed, jnp.zeros_like(handed))
    returned = lax.all_to_all(sending_back, "grp", split_axis=0, concat_axis=0, tiled=True)
    back = lax.dynamic_slice_in_dim(returned, target, 1, 0)
    grad_clips = jnp.concatenate([grad_work[0:1], back], axis=0)
    return (outputs, grad_clips)


def solution(mesh):
    in_specs = (P("grp", None, "sp", None), P(), P(), P(), P(), P("grp", None, "sp", None))
    out_specs = (P("grp", None, "sp", None), P("grp", None, "sp", None))
    return jax.shard_map(
        on_device, mesh=mesh, in_specs=in_specs, out_specs=out_specs, check_vma=False
    )
```

profile of v0, /device:TPU:1, one launch (start us, length us, event | category | flops | bytes accessed | tf_op | source)
XLA Modules:
  0.0 603.3 jit_solution(5556414309901035178)
XLA Ops:
  8.6 7.8 %all-to-all-start = ((bf16[16,8,32,1152]{3,2,1,0:T(8,128)(2,1)}), bf16[16,8,32,1152]{3,2,1,0:T(8,128)(2,1)}, u32[]{:S(2)}, u32[]{:S(2)}) async-start(bf16[16,8,32,1152]{3,2,1,0:T(8,128)(2,1)} %broadcast_select_fusion.1), calls=%async_computation | async-start | bytes 18874368 | tf_op jit(solution)/shard_map/all_to_all | solution.py:35
  25.4 5.7 reshape.89
  35.2 119.8 %all-to-all-done = bf16[16,8,32,1152]{3,2,1,0:T(8,128)(2,1)} async-done(((bf16[16,8,32,1152]{3,2,1,0:T(8,128)(2,1)}), bf16[16,8,32,1152]{3,2,1,0:T(8,128)(2,1)}, u32[]{:S(2)}, u32[]{:S(2)}) %all-to-all-start) | async-done | bytes 9437216 | tf_op jit(solution)/shard_map/all_to_all | solution.py:35
  155.0 7.1 %all-to-all-start.3 = ((bf16[2,8,32,16,72]{4,2,1,0,3:T(8,128)(2,1)}), bf16[2,8,32,16,72]{4,2,1,0,3:T(8,128)(2,1)}, u32[]{:S(2)}, u32[]{:S(2)}) async-start(bf16[2,8,32,16,72]{4,2,1,0,3:T(8,128)(2,1)} %copy.54), calls=%async_computation.3 | async-start | bytes 4194304 | tf_op jit(solution)/shard_map/all_to_all | solution.py:65
  164.1 9.8 %fusion.8 = bf16[2,8,32,3456]{3,2,1,0:T(8,128)(2,1)} fusion(bf16[1152,3456]{1,0:T(8,128)(2,1)} %param.9, f32[2,8,32]{2,1,0:T(8,128)S(1)} %fusion.47, f32[2,8,32]{2,1,0:T(8,128)S(1)} %broadcast_multiply_fusion, bf16[1,8,32,1152]{3,2,1,0:T(8,128)(2,1)S(1)} %constant_dynamic-slice_fusion.1, bf16[1,8,32,1152]{3,2,1,0:T(8,128)(2,1)S(1)} %get-tuple-element.10), kind=kOutput, calls=%fused_computation.18 | convolution fusion | flops 4081582080 | bytes 12685312 | tf_op jit(solution)/shard_map/dot_general | solution.py:45
  173.9 13.6 %reshape.87 = bf16[2,8,32,3,16,72]{5,4,3,2,1,0:T(8,128)(2,1)} reshape(bf16[2,8,32,3456]{3,2,1,0:T(8,128)(2,1)} %fusion.8) | data formatting | bytes 7077888 | tf_op jit(solution)/shard_map/reshape | solution.py:48
  187.5 7.1 %copy.44 = bf16[2,8,32,3,16,72]{5,2,3,1,0,4:T(8,128)(2,1)} copy(bf16[2,8,32,3,16,72]{5,4,3,2,1,0:T(8,128)(2,1)} %reshape.87) | data formatting | bytes 7077888 | tf_op jit(solution)/shard_map/reshape | solution.py:48
  194.6 5.1 all-to-all-start.1
  206.9 64.1 %all-to-all-done.1 = bf16[2,8,32,3,16,72]{5,2,3,1,0,4:T(8,128)(2,1)} async-done(((bf16[2,8,32,3,16,72]{5,2,3,1,0,4:T(8,128)(2,1)}), bf16[2,8,32,3,16,72]{5,2,3,1,0,4:T(8,128)(2,1)}, u32[]{:S(2)}, u32[]{:S(2)}) %all-to-all-start.1) | async-done | bytes 3538976 | tf_op jit(solution)/shard_map/all_to_all | solution.py:49
  279.0 5.8 convert_reduce_fusion
  284.8 6.8 %fusion.54 = (f32[2,8,2,256]{3,2,1,0:T(2,128)S(1)}, f32[2,8,2,256,256]{3,4,2,1,0:T(8,128)S(1)}, bf16[2,8,2,256,256]{3,4,2,1,0:T(8,128)(2,1)}) fusion(f32[2,8,2,256]{3,2,1,0:T(2,128)S(1)} %get-tuple-element.14, f32[2,8,2,256,256]{3,4,2,1,0:T(8,128)S(1)} %get-tuple-element.15, f32[2,8,2,256]{3,2,1,0:T(2,128)S(1)} %neg.12, f32[2,8,2,256]{3,2,1,0:T(2,128)S(1)} %fusion.19, ...), kind=kLoop, calls=%fused_computation.91 | loop fusion | flops 18866176 | bytes 25296896 | tf_op jit(solution)/shard_map/transpose(jvp())/reduce_sum | solution.py:21
  307.2 15.9 %copy.61 = bf16[2,8,256,3,2,72]{5,4,1,0,3,2:T(2,128)(2,1)} copy(bf16[2,8,256,3,2,72]{2,5,4,1,0,3:T(8,128)(2,1)} %pad_maximum_fusion) | data formatting | bytes 7077888 | tf_op jit(solution)/shard_map/stack | solution.py:67
  323.1 5.5 all-to-all-start.4
  329.3 4.7 fusion.39
  333.9 6.0 copy.51
  339.9 60.0 %all-to-all-done.4 = bf16[2,8,256,3,2,72]{5,4,1,0,3,2:T(2,128)(2,1)} async-done(((bf16[2,8,256,3,2,72]{5,4,1,0,3,2:T(2,128)(2,1)}), bf16[2,8,256,3,2,72]{5,4,1,0,3,2:T(2,128)(2,1)}, u32[]{:S(2)}, u32[]{:S(2)}) %all-to-all-start.4) | async-done | bytes 3538976 | tf_op jit(solution)/shard_map/all_to_all | solution.py:68
  400.0 5.3 all-to-all-start.2
  405.3 5.2 copy.62
  410.5 6.1 %copy.63 = bf16[2,8,32,3,8,2,72]{6,5,4,3,2,1,0:T(2,128)(2,1)} copy(bf16[2,8,32,3,8,2,72]{6,2,4,5,3,1,0:T(8,128)(2,1)S(1)} %bitcast.110) | data formatting | bytes 7077888 | tf_op jit(solution)/shard_map/all_to_all | solution.py:68
  416.6 18.7 %reshape.90 = bf16[2,8,32,3456]{3,2,1,0:T(8,128)(2,1)} reshape(bf16[2,8,32,3,8,2,72]{6,5,4,3,2,1,0:T(2,128)(2,1)} %copy.63) | data formatting | bytes 7077888 | tf_op jit(solution)/shard_map/reshape | solution.py:69
  435.3 9.4 %fusion.30 = (f32[2,8,32]{2,1,0:T(8,128)S(1)}, f32[2,8,32,1152]{3,2,1,0:T(8,128)S(1)}) fusion(f32[2,8,32]{2,1,0:T(8,128)S(1)} %broadcast_multiply_fusion, bf16[1,8,32,1152]{3,2,1,0:T(8,128)(2,1)} %copy-done.4, bf16[1,8,32,1152]{3,2,1,0:T(8,128)(2,1)S(1)} %copy-done.3, bf16[2,8,32,3456]{3,2,1,0:T(8,128)(2,1)} %reshape.90, bf16[1152,3456]{1,0:T(8,128)(2,1)} %param.9), kind=kOutput, calls=%fused_computation.45 | convolution fusion | flops 4079812096 | bytes 15044608 | tf_op jit(solution)/shard_map/cfse,de->cfsd/dot_general | solution.py:70
  452.4 5.6 all-to-all-start.5
  465.8 7.4 %reshape.88 = bf16[2,8,32,1152]{3,2,1,0:T(8,128)(2,1)} reshape(bf16[2,8,32,8,2,72]{5,4,3,2,1,0:T(2,128)(2,1)} %copy.53) | data formatting | bytes 2359296 | tf_op jit(solution)/shard_map/reshape | solution.py:57
  477.4 122.4 %all-to-all-done.5 = bf16[16,8,32,1152]{3,2,1,0:T(8,128)(2,1)} async-done(((bf16[16,8,32,1152]{3,2,1,0:T(8,128)(2,1)}), bf16[16,8,32,1152]{3,2,1,0:T(8,128)(2,1)}, u32[]{:S(2)}, u32[]{:S(2)}) %all-to-all-start.5) | async-done | bytes 9437216 | tf_op jit(solution)/shard_map/all_to_all | solution.py:76
  (65 shorter events, 72.6 us)
Async XLA Ops:
  0.6 20.6 %copy-start = (bf16[1152,1152]{1,0:T(8,128)(2,1)S(1)}, bf16[1152,1152]{1,0:T(8,128)(2,1)}, u32[]{:S(2)}) copy-start(bf16[1152,1152]{1,0:T(8,128)(2,1)} %param.10) | copy-start | bytes 7962628
  4.1 159.9 %copy-start.2 = (bf16[1,8,32,1152]{3,2,1,0:T(8,128)(2,1)}, bf16[1,8,32,1152]{3,2,1,0:T(8,128)(2,1)S(1)}, u32[]{:S(2)}) copy-start(bf16[1,8,32,1152]{3,2,1,0:T(8,128)(2,1)S(1)} %get-tuple-element.10) | copy-start | bytes 1769476
  8.6 7.8 %copy-start.11 = (s32[16]{0:T(128)S(1)}, s32[16]{0:T(128)}, u32[]{:S(2)}) copy-start(s32[16]{0:T(128)} %param.8) | copy-start | bytes 196
  8.6 10.6 %copy-start.10 = (s32[32]{0:T(128)S(1)}, s32[32]{0:T(128)}, u32[]{:S(2)}) copy-start(s32[32]{0:T(128)} %param.7) | copy-start | bytes 388
  8.6 146.4 %all-to-all-start = ((bf16[16,8,32,1152]{3,2,1,0:T(8,128)(2,1)}), bf16[16,8,32,1152]{3,2,1,0:T(8,128)(2,1)}, u32[]{:S(2)}, u32[]{:S(2)}) async-start(bf16[16,8,32,1152]{3,2,1,0:T(8,128)(2,1)} %broadcast_select_fusion.1), calls=%async_computation | async-start | bytes 18874368 | tf_op jit(solution)/shard_map/all_to_all | solution.py:35
  155.0 39.6 %all-to-all-start.3 = ((bf16[2,8,32,16,72]{4,2,1,0,3:T(8,128)(2,1)}), bf16[2,8,32,16,72]{4,2,1,0,3:T(8,128)(2,1)}, u32[]{:S(2)}, u32[]{:S(2)}) async-start(bf16[2,8,32,16,72]{4,2,1,0,3:T(8,128)(2,1)} %copy.54), calls=%async_computation.3 | async-start | bytes 4194304 | tf_op jit(solution)/shard_map/all_to_all | solution.py:65
  163.3 0.8 copy-start.4
  194.6 76.5 %all-to-all-start.1 = ((bf16[2,8,32,3,16,72]{5,2,3,1,0,4:T(8,128)(2,1)}), bf16[2,8,32,3,16,72]{5,2,3,1,0,4:T(8,128)(2,1)}, u32[]{:S(2)}, u32[]{:S(2)}) async-start(bf16[2,8,32,3,16,72]{5,2,3,1,0,4:T(8,128)(2,1)} %copy.44), calls=%async_computation.1 | async-start | bytes 12582912 | tf_op jit(solution)/shard_map/all_to_all | solution.py:49
  275.6 20.7 %copy-start.1 = (bf16[2,8,8,32,3,2,72]{6,3,2,5,4,1,0:T(8,128)(2,1)}, bf16[2,8,8,32,3,2,72]{6,3,2,5,4,1,0:T(8,128)(2,1)S(1)}, u32[]{:S(2)}) copy-start(bf16[2,8,8,32,3,2,72]{6,3,2,5,4,1,0:T(8,128)(2,1)S(1)} %copy.46) | copy-start | bytes 10616836
  276.9 2.1 copy-start.6
  300.9 4.1 copy-start.7
  300.9 4.1 copy-start.8
  323.1 76.9 %all-to-all-start.4 = ((bf16[2,8,256,3,2,72]{5,4,1,0,3,2:T(2,128)(2,1)}), bf16[2,8,256,3,2,72]{5,4,1,0,3,2:T(2,128)(2,1)}, u32[]{:S(2)}, u32[]{:S(2)}) async-start(bf16[2,8,256,3,2,72]{5,4,1,0,3,2:T(2,128)(2,1)} %copy.61), calls=%async_computation.4 | async-start | bytes 12582912 | tf_op jit(solution)/shard_map/all_to_all | solution.py:68
  400.0 52.5 %all-to-all-start.2 = ((bf16[2,8,256,2,72]{4,3,1,0,2:T(2,128)(2,1)}), bf16[2,8,256,2,72]{4,3,1,0,2:T(2,128)(2,1)}, u32[]{:S(2)}, u32[]{:S(2)}) async-start(bf16[2,8,256,2,72]{4,3,1,0,2:T(2,128)(2,1)} %copy.51), calls=%async_computation.2 | async-start | bytes 4194304 | tf_op jit(solution)/shard_map/all_to_all | solution.py:53
  416.6 18.7 %copy-start.3 = (bf16[1,8,32,1152]{3,2,1,0:T(8,128)(2,1)S(1)}, bf16[1,8,32,1152]{3,2,1,0:T(8,128)(2,1)}, u32[]{:S(2)}) copy-start(bf16[1,8,32,1152]{3,2,1,0:T(8,128)(2,1)} %copy-done.2) | copy-start | bytes 1769476
  435.3 9.4 %copy-start.5 = (bf16[1,8,32,1152]{3,2,1,0:T(8,128)(2,1)S(1)}, bf16[1,8,32,1152]{3,2,1,0:T(8,128)(2,1)}, u32[]{:S(2)}) copy-start(bf16[1,8,32,1152]{3,2,1,0:T(8,128)(2,1)} %copy-done.4) | copy-start | bytes 1769476
  444.7 1.3 copy-start.9
  452.4 147.4 %all-to-all-start.5 = ((bf16[16,8,32,1152]{3,2,1,0:T(8,128)(2,1)}), bf16[16,8,32,1152]{3,2,1,0:T(8,128)(2,1)}, u32[]{:S(2)}, u32[]{:S(2)}) async-start(bf16[16,8,32,1152]{3,2,1,0:T(8,128)(2,1)} %broadcast_select_fusion), calls=%async_computation.5 | async-start | bytes 18874368 | tf_op jit(solution)/shard_map/all_to_all | solution.py:76
where the time goes:
time: 613 us; the launch traced here: 603 us
  waiting for transfers between devices  366 us (60%)
  local copies, waits for them, and re-layouts  115 us (19%)
  matrix products  52.7 us (9%)
  starting transfers between devices  36.5 us (6%)
  other arithmetic  27.6 us (5%)
    all_to_all x1, waiting for transfers between devices, on_device(): lax.all_to_all(sending_back, 'grp', split_axis=0, concat_axis=0, tiled=True)  122 us
    all_to_all x1, waiting for transfers between devices, on_device(): lax.all_to_all(sending, 'grp', split_axis=0, concat_axis=0, tiled=True)  120 us
    all_to_all x1, waiting for transfers between devices, on_device(): lax.all_to_all(qkv, 'sp', split_axis=4, concat_axis=2, tiled=True)  64.1 us
    all_to_all x1, waiting for transfers between devices, on_device(): lax.all_to_all(grad_qkv, 'sp', split_axis=2, concat_axis=4, tiled=True)  60 us
    reshape x2, local copies, waits for them, and re-layouts, on_device(): qkv = qkv.reshape(work.shape[:-1] + (3, HEADS, head_dim))  20.7 us
    reshape x1, local copies, waits for them, and re-layouts, on_device(): grad_qkv = grad_qkv.reshape(work.shape[:-1] + (3 * width,))  18.7 us
    another operation x1, local copies, waits for them, and re-layouts, on_device(): grad_qkv = jnp.stack([grad_q, grad_k, grad_v], axis=-3)  15.9 us
    dot_general x3, matrix products, attend(): jnp.einsum('...hqk,...khe->...qhe', probs, values, preferred_element_type...  14.5 us
  transfers between devices with their start and end apart: 6, of which 4 were waited for; matrix products, arithmetic and copies ran while one was open for 22% of the time, Pallas kernels for 0%

commit v1 on v0

v1 whole, which is shorter than its diff:
```python
import functools
import jax
import jax.numpy as jnp
from jax import lax
from jax.experimental import pallas as pl
from jax.experimental.pallas import tpu as pltpu
from jax.sharding import PartitionSpec as P

HEADS = 16
HP = 80
GROUPS = 4
EPS = 1e-06
F32 = jnp.float32
BF16 = jnp.bfloat16
LOG2E = 1.4426950408889634
VMEM_LIMIT = 60 * 1024 * 1024


def dot_nn(a, b):
    return lax.dot_general(a, b, (((1,), (0,)), ((), ())), preferred_element_type=F32)


def dot_nt(a, b):
    return lax.dot_general(a, b, (((1,), (1,)), ((), ())), preferred_element_type=F32)


def dot_tn(a, b):
    return lax.dot_general(a, b, (((0,), (0,)), ((), ())), preferred_element_type=F32)


def forward_kernel(scale, x_ref, keep_ref, wt_hbm, wo_hbm, out_ref, qkv_hbm, p_hbm,
                   wt, wo, nrm, qkv, probs, att, wsem, osem, qsem, psem):
    toks = x_ref.shape[0]
    frames = toks // 256
    per = HEADS // GROUPS
    rows = 3 * HP * per

    def weight(g):
        return pltpu.make_async_copy(wt_hbm.at[pl.ds(g * rows, rows)], wt.at[pl.ds(g * rows, rows)], wsem.at[g])

    out_weight = pltpu.make_async_copy(wo_hbm, wo, osem)
    for g in range(GROUPS):
        weight(g).start()
    out_weight.start()
    x = x_ref[...].astype(F32)
    mean = jnp.mean(x, axis=-1, keepdims=True)
    centered = x - mean
    var = jnp.mean(centered * centered, axis=-1, keepdims=True)
    nrm[...] = (centered * lax.rsqrt(var + EPS)).astype(BF16)
    copies = []
    for g in range(GROUPS):
        weight(g).wait()
        part = pl.ds(g * rows, rows)
        qkv[part, :] = dot_nt(wt[part, :], nrm[...]).astype(BF16)
        copy = pltpu.make_async_copy(qkv.at[part], qkv_hbm.at[part], qsem.at[g])
        copy.start()
        copies.append(copy)
        for h in range(g * per, (g + 1) * per):
            for f in range(frames):
                cols = pl.ds(f * 256, 256)
                q = qkv[pl.ds(3 * HP * h, HP), cols]
                k = qkv[pl.ds(3 * HP * h + HP, HP), cols]
                v = qkv[pl.ds(3 * HP * h + 2 * HP, HP), cols]
                s = dot_tn(k, q)
                top = jnp.max(s, axis=0, keepdims=True)
                e = jnp.exp2((s - top) * (scale * LOG2E))
                p = (e * (1.0 / jnp.sum(e, axis=0, keepdims=True))).astype(BF16)
                probs[h, :, cols] = p
                att[pl.ds(HP * h, HP), cols] = dot_nn(v, p).astype(BF16)
        part = pl.ds(g * per, per)
        copy = pltpu.make_async_copy(probs.at[part], p_hbm.at[part], psem.at[g])
        copy.start()
        copies.append(copy)
    out_weight.wait()
    projected = dot_tn(att[...], wo[...])
    out_ref[...] = jnp.where(keep_ref[...] > 0, x_ref[...].astype(F32) + projected, 0.0).astype(BF16)
    for copy in copies:
        copy.wait()


def forward(x, keep, wt, wo, scale):
    toks, width = x.shape
    return pl.pallas_call(
        functools.partial(forward_kernel, scale),
        out_shape=(
            jax.ShapeDtypeStruct((toks, width), BF16),
            jax.ShapeDtypeStruct((wt.shape[0], toks), BF16),
            jax.ShapeDtypeStruct((HEADS, 256, toks), BF16),
        ),
        in_specs=[pl.BlockSpec(memory_space=pltpu.VMEM)] * 2 + [pl.BlockSpec(memory_space=pl.ANY)] * 2,
        out_specs=(pl.BlockSpec(memory_space=pltpu.VMEM), pl.BlockSpec(memory_space=pl.ANY), pl.BlockSpec(memory_space=pl.ANY)),
        scratch_shapes=[
            pltpu.VMEM(wt.shape, BF16),
            pltpu.VMEM(wo.shape, BF16),
            pltpu.VMEM((toks, width), BF16),
            pltpu.VMEM((wt.shape[0], toks), BF16),
            pltpu.VMEM((HEADS, 256, toks), BF16),
            pltpu.VMEM((wo.shape[0], toks), BF16),
            pltpu.SemaphoreType.DMA((GROUPS,)),
            pltpu.SemaphoreType.DMA,
            pltpu.SemaphoreType.DMA((GROUPS,)),
            pltpu.SemaphoreType.DMA((GROUPS,)),
        ],
        compiler_params=pltpu.CompilerParams(vmem_limit_bytes=VMEM_LIMIT),
        name="forward",
    )(x, keep, wt, wo)


def backward_kernel(scale, x_ref, c_ref, keep_ref, wt_hbm, wo_hbm, qkv_hbm, p_hbm, out_ref,
                    wt, wo, qkv, probs, gatt, gqkv, wsem, osem, qsem, psem):
    toks = x_ref.shape[0]
    frames = toks // 256
    per = HEADS // GROUPS
    rows = 3 * HP * per

    def load_qkv(g):
        part = pl.ds(g * rows, rows)
        return pltpu.make_async_copy(qkv_hbm.at[part], qkv.at[part], qsem.at[g])

    def load_probs(g):
        part = pl.ds(g * per, per)
        return pltpu.make_async_copy(p_hbm.at[part], probs.at[part], psem.at[g])

    load_wo = pltpu.make_async_copy(wo_hbm, wo, osem)
    load_wt = pltpu.make_async_copy(wt_hbm, wt, wsem)
    load_wo.start()
    for g in range(GROUPS):
        load_qkv(g).start()
        load_probs(g).start()
    load_wt.start()
    keep = keep_ref[...] > 0
    gout = jnp.where(keep, c_ref[...], jnp.zeros_like(c_ref[...]))
    load_wo.wait()
    gatt[...] = dot_nt(wo[...], gout).astype(BF16)
    for g in range(GROUPS):
        load_qkv(g).wait()
        load_probs(g).wait()
        for h in range(g * per, (g + 1) * per):
            for f in range(frames):
                cols = pl.ds(f * 256, 256)
                at = 3 * HP * h
                q = qkv[pl.ds(at, HP), cols]
                k = qkv[pl.ds(at + HP, HP), cols]
                v = qkv[pl.ds(at + 2 * HP, HP), cols]
                p = probs[h, :, cols]
                ga = gatt[pl.ds(HP * h, HP), cols]
                gp = dot_tn(v, ga)
                pf = p.astype(F32)
                mass = jnp.sum(pf * gp, axis=0, keepdims=True)
                gs = (pf * (gp - mass) * scale).astype(BF16)
                gqkv[pl.ds(at, HP), cols] = dot_nn(k, gs).astype(BF16)
                gqkv[pl.ds(at + HP, HP), cols] = dot_nt(q, gs).astype(BF16)
                gqkv[pl.ds(at + 2 * HP, HP), cols] = dot_nt(ga, p).astype(BF16)
    load_wt.wait()
    gn = dot_tn(gqkv[...], wt[...])
    x = x_ref[...].astype(F32)
    mean = jnp.mean(x, axis=-1, keepdims=True)
    centered = x - mean
    var = jnp.mean(centered * centered, axis=-1, keepdims=True)
    inv = lax.rsqrt(var + EPS)
    n = centered * inv
    gx = inv * (gn - jnp.mean(gn, axis=-1, keepdims=True) - n * jnp.mean(gn * n, axis=-1, keepdims=True))
    gout = jnp.where(keep, c_ref[...], jnp.zeros_like(c_ref[...])).astype(F32)
    out_ref[...] = (gout + gx).astype(BF16)


def backward(x, c, keep, wt, wo, qkv, probs, scale):
    toks, width = x.shape
    return pl.pallas_call(
        functools.partial(backward_kernel, scale),
        out_shape=jax.ShapeDtypeStruct((toks, width), BF16),
        in_specs=[pl.BlockSpec(memory_space=pltpu.VMEM)] * 3 + [pl.BlockSpec(memory_space=pl.ANY)] * 4,
        out_specs=pl.BlockSpec(memory_space=pltpu.VMEM),
        scratch_shapes=[
            pltpu.VMEM(wt.shape, BF16),
            pltpu.VMEM(wo.shape, BF16),
            pltpu.VMEM(qkv.shape, BF16),
            pltpu.VMEM(probs.shape, BF16),
            pltpu.VMEM((wo.shape[0], toks), BF16),
            pltpu.VMEM(qkv.shape, BF16),
            pltpu.SemaphoreType.DMA,
            pltpu.SemaphoreType.DMA,
            pltpu.SemaphoreType.DMA((GROUPS,)),
            pltpu.SemaphoreType.DMA((GROUPS,)),
        ],
        compiler_params=pltpu.CompilerParams(vmem_limit_bytes=VMEM_LIMIT),
        name="backward",
    )(x, c, keep, wt, wo, qkv, probs)


def pad_weights(weight_qkv, weight_out):
    width = weight_out.shape[0]
    hd = width // HEADS
    wt = weight_qkv.T.reshape(3, HEADS, hd, width).transpose(1, 0, 2, 3)
    wt = jnp.pad(wt, ((0, 0), (0, 0), (0, HP - hd), (0, 0))).reshape(HEADS * 3 * HP, width)
    wo = jnp.pad(weight_out.reshape(HEADS, hd, width), ((0, 0), (0, HP - hd), (0, 0))).reshape(HEADS * HP, width)
    return wt, wo


def shuffle_kernel(index_ref, x_hbm, out_hbm, sem):
    copies = [
        pltpu.make_async_copy(x_hbm.at[index_ref[i]], out_hbm.at[i], sem.at[i]) for i in range(x_hbm.shape[0])
    ]
    for copy in copies:
        copy.start()
    for copy in copies:
        copy.wait()


def shuffle(x, index):
    return pl.pallas_call(
        shuffle_kernel,
        out_shape=jax.ShapeDtypeStruct(x.shape, x.dtype),
        in_specs=[pl.BlockSpec(memory_space=pltpu.SMEM), pl.BlockSpec(memory_space=pl.ANY)],
        out_specs=pl.BlockSpec(memory_space=pl.ANY),
        scratch_shapes=[pltpu.SemaphoreType.DMA((x.shape[0],))],
        name="shuffle",
    )(index, x)


def route(x, index, groups):
    tokens, width = x.shape
    pieces = x.reshape(groups, tokens // groups, width)
    pieces = lax.all_to_all(pieces, "grp", 0, 0, tiled=True)
    pieces = shuffle(pieces, index)
    pieces = lax.all_to_all(pieces, "grp", 0, 0, tiled=True)
    return pieces.reshape(tokens, width)


def gather_frame(x):
    frames, part, width = x.shape
    return lax.all_to_all(x, "sp", 0, 0, tiled=True).reshape(frames * part, width)


def scatter_frame(x, frames):
    tokens, width = x.shape
    return lax.all_to_all(x.reshape(frames, tokens // frames, width), "sp", 0, 0, tiled=True)


def on_device(clips, counts, dest, weight_qkv, weight_out, cotangent):
    groups = lax.axis_size("grp")
    me = lax.axis_index("grp")
    frame = lax.axis_index("sp")
    frames = clips.shape[1]
    order = jnp.arange(groups, dtype=jnp.int32)
    source = jnp.sum(jnp.where(dest[None, :] == order[:, None], order[None, :], 0), axis=1)
    scale = (weight_out.shape[0] // HEADS) ** -0.5
    wt, wo = pad_weights(weight_qkv, weight_out)
    xa = gather_frame(clips[0])
    xb = gather_frame(clips[1])
    ca = gather_frame(cotangent[0])
    cb = route(gather_frame(cotangent[1]), dest, groups)
    x = jnp.concatenate([xa, xb])
    c = jnp.concatenate([ca, cb])
    used = lax.dynamic_slice_in_dim(counts, 2 * me, 2)
    keep = jnp.repeat((frame < used).astype(F32), 256)[:, None]
    out, qkv, probs = forward(x, keep, wt, wo, scale)
    grad = backward(x, c, keep, wt, wo, qkv, probs, scale)
    oa = scatter_frame(out[:256], frames)
    ob = scatter_frame(route(out[256:], source, groups), frames)
    ga = scatter_frame(grad[:256], frames)
    gb = scatter_frame(grad[256:], frames)
    return (jnp.stack([oa, ob]), jnp.stack([ga, gb]))


def solution(mesh):
    spec = P("grp", None, "sp", None)
    return jax.shard_map(
        on_device, mesh=mesh, in_specs=(spec, P(), P(), P(), P(), spec), out_specs=(spec, spec), check_vma=False
    )
```

time: 613 us -> 271 us (0.44); the launches traced: 603 us -> 269 us
  waiting for transfers between devices: 366 us -> 36.4 us
  Pallas kernels: 0 us -> 89.1 us
  local copies, waits for them, and re-layouts: 115 us -> 35.7 us
  blocking collectives: 0 us -> 60.8 us
  matrix products: 52.7 us -> 0 us
  other arithmetic: 27.6 us -> 5.23 us
    all_to_all x6 -> x8, waiting for transfers between devices: 366 us -> 36.4 us  [the longest x4 27.3 us: gather_frame(): lax.all_to_all(x, 'sp', 0, 0, tiled=True).reshape(frames * part, width)]
    pallas_call x0 -> x4, Pallas kernels: none -> 89.1 us  [the longest x2 39.7 us: shuffle(): pl.pallas_call(shuffle_kernel, out_shape=jax.ShapeDtypeStruct(x.shape, x....]
    all_to_all x0 -> x4, blocking collectives: none -> 60.8 us  [the longest x3 42.9 us: scatter_frame(): lax.all_to_all(x.reshape(frames, tokens // frames, width), 'sp', 0, 0, ti...]
    reshape x6 -> x0, local copies, waits for them, and re-layouts: 56 us -> none  [the longest x2 20.7 us: on_device(): qkv = qkv.reshape(work.shape[:-1] + (3, HEADS, head_dim))]
    dot_general x10 -> x0, matrix products: 52.7 us -> none  [the longest x3 14.5 us: attend(): jnp.einsum('...hqk,...khe->...qhe', probs, values, preferred_element_type...]
    all_to_all x7 -> x0, local copies, waits for them, and re-layouts: 28.9 us -> none  [the longest x2 11.3 us: on_device(): lax.all_to_all(grad_qkv, 'sp', split_axis=2, concat_axis=4, tiled=True)]
    unnamed x24 -> x15, local copies, waits for them, and re-layouts: 1.21 us -> 19.5 us
    another operation x1 -> x0, local copies, waits for them, and re-layouts: 15.9 us -> none  [on_device(): grad_qkv = jnp.stack([grad_q, grad_k, grad_v], axis=-3)]
  transfers between devices with their start and end apart: 6 -> 8, of which waited for: 4 -> 4; matrix products, arithmetic and copies ran while one was open for 22% -> 14% of each run, Pallas kernels for 0% -> 33%
where the time goes in v1:
time: 271 us; the launch traced here: 269 us
  Pallas kernels  89.1 us (33%)
  blocking collectives  60.8 us (22%)
  starting transfers between devices  41.5 us (15%)
  waiting for transfers between devices  36.4 us (13%)
  local copies, waits for them, and re-layouts  35.7 us (13%)
  other arithmetic  5.23 us (2%)
    all_to_all x3, blocking collectives, scatter_frame(): lax.all_to_all(x.reshape(frames, tokens // frames, width), 'sp', 0, 0, ti...  42.9 us
    pallas_call x2, Pallas kernels, shuffle(): pl.pallas_call(shuffle_kernel, out_shape=jax.ShapeDtypeStruct(x.shape, x....  39.7 us
    all_to_all x4, waiting for transfers between devices, gather_frame(): lax.all_to_all(x, 'sp', 0, 0, tiled=True).reshape(frames * part, width)  27.3 us
    pallas_call x1, Pallas kernels, backward(): pl.pallas_call(functools.partial(backward_kernel, scale), out_shape=jax.S...  27.2 us
    pallas_call x1, Pallas kernels, forward(): pl.pallas_call(functools.partial(forward_kernel, scale), out_shape=(jax.S...  22.2 us
    all_to_all x4, starting transfers between devices, gather_frame(): lax.all_to_all(x, 'sp', 0, 0, tiled=True).reshape(frames * part, width)  20.4 us
    unnamed x15, local copies, waits for them, and re-layouts  19.5 us
    all_to_all x1, blocking collectives, route(): pieces = lax.all_to_all(pieces, 'grp', 0, 0, tiled=True)  17.9 us
  transfers between devices with their start and end apart: 8, of which 4 were waited for; matrix products, arithmetic and copies ran while one was open for 14% of the time, Pallas kernels for 33%

profile of v1, /device:TPU:1, one launch (start us, length us, event | category | flops | bytes accessed | tf_op | source)
XLA Modules:
  0.0 269.4 jit_solution(9883414974027073943)
XLA Ops:
  0.6 2.3 slice_bitcast_fusion.3
  3.0 6.9 %all-to-all-start = ((bf16[8,32,1152]{2,1,0:T(8,128)(2,1)}), bf16[8,32,1152]{2,1,0:T(8,128)(2,1)S(1)}, u32[]{:S(2)}, u32[]{:S(2)}) async-start(bf16[8,32,1152]{2,1,0:T(8,128)(2,1)} %get-tuple-element.14), calls=%async_computation | async-start | bytes 1179648 | tf_op jit(solution)/shard_map/all_to_all | solution.py:232
  9.9 10.2 %all-to-all-done = bf16[8,32,1152]{2,1,0:T(8,128)(2,1)S(1)} async-done(((bf16[8,32,1152]{2,1,0:T(8,128)(2,1)}), bf16[8,32,1152]{2,1,0:T(8,128)(2,1)S(1)}, u32[]{:S(2)}, u32[]{:S(2)}) %all-to-all-start) | async-done | bytes 589856 | tf_op jit(solution)/shard_map/all_to_all | solution.py:232
  20.1 4.3 %all-to-all-start.1 = ((bf16[8,32,1152]{2,1,0:T(8,128)(2,1)}), bf16[8,32,1152]{2,1,0:T(8,128)(2,1)S(1)}, u32[]{:S(2)}, u32[]{:S(2)}) async-start(bf16[8,32,1152]{2,1,0:T(8,128)(2,1)} %get-tuple-element.15), calls=%async_computation.1 | async-start | bytes 1179648 | tf_op jit(solution)/shard_map/all_to_all | solution.py:232
  25.5 9.1 %all-to-all-done.1 = bf16[8,32,1152]{2,1,0:T(8,128)(2,1)S(1)} async-done(((bf16[8,32,1152]{2,1,0:T(8,128)(2,1)}), bf16[8,32,1152]{2,1,0:T(8,128)(2,1)S(1)}, u32[]{:S(2)}, u32[]{:S(2)}) %all-to-all-start.1) | async-done | bytes 589856 | tf_op jit(solution)/shard_map/all_to_all | solution.py:232
  34.6 4.3 %all-to-all-start.7 = ((bf16[8,32,1152]{2,1,0:T(8,128)(2,1)}), bf16[8,32,1152]{2,1,0:T(8,128)(2,1)S(1)}, u32[]{:S(2)}, u32[]{:S(2)}) async-start(bf16[8,32,1152]{2,1,0:T(8,128)(2,1)} %get-tuple-element.11), calls=%async_computation.7 | async-start | bytes 1179648 | tf_op jit(solution)/shard_map/all_to_all | solution.py:232
  39.9 11.5 %copy.13 = bf16[1152,3456]{0,1:T(8,128)(2,1)} copy(bf16[1152,3456]{1,0:T(8,128)(2,1)} %param.9) | data formatting | bytes 15925248 | tf_op args[3]
  51.5 7.0 %copy.17 = bf16[16,3,72,1152]{3,2,1,0:T(8,128)(2,1)} copy(bf16[16,3,72,1152]{3,2,0,1:T(8,128)(2,1)} %bitcast.37) | data formatting | bytes 15925248
  58.5 7.5 %pad.8.clone = bf16[16,3,80,1152]{3,2,1,0:T(8,128)(2,1)} pad(bf16[16,3,72,1152]{3,2,1,0:T(8,128)(2,1)} %copy.17, bf16[]{:T(256)} %constant.16.clone.1), padding=0_0x0_0x0_8x0_0 | pad | bytes 16809986 | tf_op jit(solution)/shard_map/jit(_pad)/pad | solution.py:195
  68.9 22.2 %forward.1 = (bf16[512,1152]{1,0:T(8,128)(2,1)}, bf16[3840,512]{1,0:T(8,128)(2,1)}, bf16[16,256,512]{2,1,0:T(8,128)(2,1)}) custom-call(bf16[512,1152]{1,0:T(8,128)(2,1)} %pad_maximum_fusion.x_ref, f32[512,1]{1,0:T(8,128)} %bitcast.41, bf16[3840,1152]{1,0:T(8,128)(2,1)} %bitcast.35, bf16[1280,1152]{1,0:T(8,128)(2,1)} %bitcast.38), custom_call_target="tpu_custom_call" | custom-call | tf_op jit(solution)/shard_map/forward/pallas_call | solution.py:83
  91.0 4.8 %all-to-all-start.6 = ((bf16[8,32,1152]{2,1,0:T(8,128)(2,1)}), bf16[8,32,1152]{2,1,0:T(8,128)(2,1)S(1)}, u32[]{:S(2)}, u32[]{:S(2)}) async-start(bf16[8,32,1152]{2,1,0:T(8,128)(2,1)} %get-tuple-element.10), calls=%async_computation.6 | async-start | bytes 1179648 | tf_op jit(solution)/shard_map/all_to_all | solution.py:232
  98.0 8.0 %all-to-all-done.6 = bf16[8,32,1152]{2,1,0:T(8,128)(2,1)S(1)} async-done(((bf16[8,32,1152]{2,1,0:T(8,128)(2,1)}), bf16[8,32,1152]{2,1,0:T(8,128)(2,1)S(1)}, u32[]{:S(2)}, u32[]{:S(2)}) %all-to-all-start.6) | async-done | bytes 589856 | tf_op jit(solution)/shard_map/all_to_all | solution.py:232
  106.1 13.6 %all_to_all.60 = bf16[8,32,1152]{2,1,0:T(8,128)(2,1)S(1)} all-to-all(bf16[8,32,1152]{2,1,0:T(8,128)(2,1)S(1)} %bitcast.52), channel_id=1, replica_groups=mesh['grp'=16,'sp'=8] {'sp'}, dimensions={0} | all-to-all | bytes 1179648 | tf_op jit(solution)/shard_map/all_to_all | solution.py:237
  119.7 17.9 %all_to_all.61.x_hbm = bf16[16,16,1152]{2,1,0:T(8,128)(2,1)} all-to-all(bf16[16,16,1152]{2,1,0:T(8,128)(2,1)S(1)} %bitcast.43), channel_id=1, replica_groups=mesh['grp'=16,'sp'=8] {'grp'}, dimensions={0} | all-to-all | bytes 1179648 | tf_op jit(solution)/shard_map/all_to_all | solution.py:224
  137.5 3.6 %all-to-all-start.3 = ((bf16[16,16,1152]{2,1,0:T(8,128)(2,1)}), bf16[16,16,1152]{2,1,0:T(8,128)(2,1)S(1)}, u32[]{:S(2)}, u32[]{:S(2)}) async-start(bf16[16,16,1152]{2,1,0:T(8,128)(2,1)} %bitcast.12), calls=%async_computation.3 | async-start | bytes 1179648 | tf_op jit(solution)/shard_map/all_to_all | solution.py:224
  141.2 19.9 %shuffle.3 = bf16[16,16,1152]{2,1,0:T(8,128)(2,1)} custom-call(s32[16]{0:T(128)} %index_ref.1, bf16[16,16,1152]{2,1,0:T(8,128)(2,1)} %all_to_all.61.x_hbm), custom_call_target="tpu_custom_call" | custom-call | tf_op jit(solution)/shard_map/shuffle/pallas_call | solution.py:211
  161.1 6.6 %all-to-all-start.9 = ((bf16[16,16,1152]{2,1,0:T(8,128)(2,1)}), bf16[16,16,1152]{2,1,0:T(8,128)(2,1)S(1)}, u32[]{:S(2)}, u32[]{:S(2)}) async-start(bf16[16,16,1152]{2,1,0:T(8,128)(2,1)} %shuffle.3), calls=%async_computation.9 | async-start | bytes 1179648 | tf_op jit(solution)/shard_map/all_to_all | solution.py:226
  168.4 19.8 %shuffle.2 = bf16[16,16,1152]{2,1,0:T(8,128)(2,1)} custom-call(s32[16]{0:T(128)} %select_reduce_fusion.index_ref, bf16[16,16,1152]{2,1,0:T(8,128)(2,1)} %copy-done.1), custom_call_target="tpu_custom_call" | custom-call | tf_op jit(solution)/shard_map/shuffle/pallas_call | solution.py:211
  188.2 6.7 %all-to-all-start.4 = ((bf16[16,16,1152]{2,1,0:T(8,128)(2,1)}), bf16[16,16,1152]{2,1,0:T(8,128)(2,1)}, u32[]{:S(2)}, u32[]{:S(2)}) async-start(bf16[16,16,1152]{2,1,0:T(8,128)(2,1)} %shuffle.2), calls=%async_computation.4 | async-start | bytes 1179648 | tf_op jit(solution)/shard_map/all_to_all | solution.py:226
  196.0 27.2 %backward.1 = bf16[512,1152]{1,0:T(8,128)(2,1)} custom-call(bf16[512,1152]{1,0:T(8,128)(2,1)} %pad_maximum_fusion.x_ref, bf16[512,1152]{1,0:T(8,128)(2,1)} %pad_maximum_fusion.2.c_ref, f32[512,1]{1,0:T(8,128)} %bitcast.42, bf16[3840,1152]{1,0:T(8,128)(2,1)} %bitcast.36, bf16[1280,1152]{1,0:T(8,128)(2,1)} %bitcast.39, ...), custom_call_target="tpu_custom_call" | custom-call | tf_op jit(solution)/shard_map/backward/pallas_call | solution.py:169
  224.6 15.8 %all_to_all.62 = bf16[8,32,1152]{2,1,0:T(8,128)(2,1)S(1)} all-to-all(bf16[8,32,1152]{2,1,0:T(8,128)(2,1)S(1)} %bitcast.53), channel_id=1, replica_groups=mesh['grp'=16,'sp'=8] {'sp'}, dimensions={0} | all-to-all | bytes 1179648 | tf_op jit(solution)/shard_map/all_to_all | solution.py:237
  240.4 13.5 %all_to_all.63 = bf16[8,32,1152]{2,1,0:T(8,128)(2,1)S(1)} all-to-all(bf16[8,32,1152]{2,1,0:T(8,128)(2,1)S(1)} %bitcast.50), channel_id=1, replica_groups=mesh['grp'=16,'sp'=8] {'sp'}, dimensions={0} | all-to-all | bytes 1179648 | tf_op jit(solution)/shard_map/all_to_all | solution.py:237
  253.9 4.2 %all-to-all-start.5 = ((bf16[8,32,1152]{2,1,0:T(8,128)(2,1)}), bf16[8,32,1152]{2,1,0:T(8,128)(2,1)S(1)}, u32[]{:S(2)}, u32[]{:S(2)}) async-start(bf16[8,32,1152]{2,1,0:T(8,128)(2,1)} %bitcast.13), calls=%async_computation.5 | async-start | bytes 1179648 | tf_op jit(solution)/shard_map/all_to_all | solution.py:237
  259.2 9.1 %all-to-all-done.5 = bf16[8,32,1152]{2,1,0:T(8,128)(2,1)S(1)} async-done(((bf16[8,32,1152]{2,1,0:T(8,128)(2,1)}), bf16[8,32,1152]{2,1,0:T(8,128)(2,1)S(1)}, u32[]{:S(2)}, u32[]{:S(2)}) %all-to-all-start.5) | async-done | bytes 589856 | tf_op jit(solution)/shard_map/all_to_all | solution.py:237
  (27 shorter events, 12.6 us)
Async XLA Ops:
  3.0 21.4 %copy-start.2 = (bf16[2,8,32,1152]{3,2,1,0:T(8,128)(2,1)S(1)}, bf16[2,8,32,1152]{3,2,1,0:T(8,128)(2,1)}, u32[]{:S(2)}) copy-start(bf16[2,8,32,1152]{3,2,1,0:T(8,128)(2,1)} %param.11) | copy-start | bytes 3538948
  3.0 17.1 %all-to-all-start = ((bf16[8,32,1152]{2,1,0:T(8,128)(2,1)}), bf16[8,32,1152]{2,1,0:T(8,128)(2,1)S(1)}, u32[]{:S(2)}, u32[]{:S(2)}) async-start(bf16[8,32,1152]{2,1,0:T(8,128)(2,1)} %get-tuple-element.14), calls=%async_computation | async-start | bytes 1179648 | tf_op jit(solution)/shard_map/all_to_all | solution.py:232
  20.1 14.5 %all-to-all-start.1 = ((bf16[8,32,1152]{2,1,0:T(8,128)(2,1)}), bf16[8,32,1152]{2,1,0:T(8,128)(2,1)S(1)}, u32[]{:S(2)}, u32[]{:S(2)}) async-start(bf16[8,32,1152]{2,1,0:T(8,128)(2,1)} %get-tuple-element.15), calls=%async_computation.1 | async-start | bytes 1179648 | tf_op jit(solution)/shard_map/all_to_all | solution.py:232
  25.5 13.4 %copy-start.4 = (s32[32]{0:T(128)S(1)}, s32[32]{0:T(128)}, u32[]{:S(2)}) copy-start(s32[32]{0:T(128)} %param.7) | copy-start | bytes 388
  34.6 56.4 %all-to-all-start.7 = ((bf16[8,32,1152]{2,1,0:T(8,128)(2,1)}), bf16[8,32,1152]{2,1,0:T(8,128)(2,1)S(1)}, u32[]{:S(2)}, u32[]{:S(2)}) async-start(bf16[8,32,1152]{2,1,0:T(8,128)(2,1)} %get-tuple-element.11), calls=%async_computation.7 | async-start | bytes 1179648 | tf_op jit(solution)/shard_map/all_to_all | solution.py:232
  58.5 7.5 %copy-start = (bf16[1152,1152]{1,0:T(8,128)(2,1)S(1)}, bf16[1152,1152]{1,0:T(8,128)(2,1)}, u32[]{:S(2)}) copy-start(bf16[1152,1152]{1,0:T(8,128)(2,1)} %param.10) | copy-start | bytes 7962628
  91.0 15.0 %all-to-all-start.6 = ((bf16[8,32,1152]{2,1,0:T(8,128)(2,1)}), bf16[8,32,1152]{2,1,0:T(8,128)(2,1)S(1)}, u32[]{:S(2)}, u32[]{:S(2)}) async-start(bf16[8,32,1152]{2,1,0:T(8,128)(2,1)} %get-tuple-element.10), calls=%async_computation.6 | async-start | bytes 1179648 | tf_op jit(solution)/shard_map/all_to_all | solution.py:232
  137.5 23.5 %all-to-all-start.3 = ((bf16[16,16,1152]{2,1,0:T(8,128)(2,1)}), bf16[16,16,1152]{2,1,0:T(8,128)(2,1)S(1)}, u32[]{:S(2)}, u32[]{:S(2)}) async-start(bf16[16,16,1152]{2,1,0:T(8,128)(2,1)} %bitcast.12), calls=%async_computation.3 | async-start | bytes 1179648 | tf_op jit(solution)/shard_map/all_to_all | solution.py:224
  141.1 26.6 %copy-start.3 = (s32[16]{0:T(128)S(1)}, s32[16]{0:T(128)}, u32[]{:S(2)}) copy-start(s32[16]{0:T(128)} %index_ref.1) | copy-start | bytes 196
  161.1 7.3 %copy-start.1 = (bf16[16,16,1152]{2,1,0:T(8,128)(2,1)}, bf16[16,16,1152]{2,1,0:T(8,128)(2,1)S(1)}, u32[]{:S(2)}) copy-start(bf16[16,16,1152]{2,1,0:T(8,128)(2,1)S(1)} %all-to-all-done.3.x_hbm) | copy-start | bytes 1769476
  161.1 27.1 %all-to-all-start.9 = ((bf16[16,16,1152]{2,1,0:T(8,128)(2,1)}), bf16[16,16,1152]{2,1,0:T(8,128)(2,1)S(1)}, u32[]{:S(2)}, u32[]{:S(2)}) async-start(bf16[16,16,1152]{2,1,0:T(8,128)(2,1)} %shuffle.3), calls=%async_computation.9 | async-start | bytes 1179648 | tf_op jit(solution)/shard_map/all_to_all | solution.py:226
  188.2 36.4 %all-to-all-start.4 = ((bf16[16,16,1152]{2,1,0:T(8,128)(2,1)}), bf16[16,16,1152]{2,1,0:T(8,128)(2,1)}, u32[]{:S(2)}, u32[]{:S(2)}) async-start(bf16[16,16,1152]{2,1,0:T(8,128)(2,1)} %shuffle.2), calls=%async_computation.4 | async-start | bytes 1179648 | tf_op jit(solution)/shard_map/all_to_all | solution.py:226
  253.9 14.4 %all-to-all-start.5 = ((bf16[8,32,1152]{2,1,0:T(8,128)(2,1)}), bf16[8,32,1152]{2,1,0:T(8,128)(2,1)S(1)}, u32[]{:S(2)}, u32[]{:S(2)}) async-start(bf16[8,32,1152]{2,1,0:T(8,128)(2,1)} %bitcast.13), calls=%async_computation.5 | async-start | bytes 1179648 | tf_op jit(solution)/shard_map/all_to_all | solution.py:237

commit v2 on v0

v2 whole, which is shorter than its diff:
```python
import functools
import jax
import jax.numpy as jnp
from jax import lax
from jax.experimental import pallas as pl
from jax.experimental.pallas import tpu as pltpu
from jax.sharding import PartitionSpec as P

HEADS = 16
HP = 80
GROUPS = 4
EPS = 1e-06
F32 = jnp.float32
BF16 = jnp.bfloat16
LOG2E = 1.4426950408889634
MIB = 1024 * 1024
IN_VMEM = pl.BlockSpec(memory_space=pltpu.VMEM)
IN_SMEM = pl.BlockSpec(memory_space=pltpu.SMEM)
ANYWHERE = pl.BlockSpec(memory_space=pltpu.HBM)


def dot_nn(a, b):
    return lax.dot_general(a, b, (((1,), (0,)), ((), ())), preferred_element_type=F32)


def dot_nt(a, b):
    return lax.dot_general(a, b, (((1,), (1,)), ((), ())), preferred_element_type=F32)


def dot_tn(a, b):
    return lax.dot_general(a, b, (((0,), (0,)), ((), ())), preferred_element_type=F32)


def cost(flops, moved):
    return pl.CostEstimate(flops=flops, bytes_accessed=moved, transcendentals=0)


def far(x):
    return pltpu.with_memory_space_constraint(x, pltpu.HBM)


def copy_all(pairs, sems):
    copies = [pltpu.make_async_copy(src, dst, sems.at[n]) for n, (src, dst) in enumerate(pairs)]
    for copy in copies:
        copy.start()
    return copies


def wait_all(copies):
    for copy in copies:
        copy.wait()


def prepare_kernel(wq_hbm, wo_hbm, wt_hbm, wop_hbm, wt_ref, wop_ref, out_sems, wq, wo, sems):
    width = wo.shape[0]
    hd = width // HEADS
    loads = [
        pltpu.make_async_copy(wq_hbm.at[:, pl.ds(j * width, width)], wq.at[j], sems.at[j]) for j in range(3)
    ]
    loads.append(pltpu.make_async_copy(wo_hbm, wo, sems.at[3]))
    for load in loads:
        load.start()
    pad = jnp.zeros((HP - hd, width), F32)

    def put(dst, rows, j):
        for h in range(HEADS):
            part = jnp.concatenate([rows[h * hd:(h + 1) * hd], pad])
            dst[pl.ds((j * HEADS + h) * HP, HP), :] = part.astype(BF16)

    saves = []
    for j in range(3):
        loads[j].wait()
        put(wt_ref, wq[j].astype(F32).T, j)
        part = pl.ds(j * HEADS * HP, HEADS * HP)
        saves.append(pltpu.make_async_copy(wt_ref.at[part], wt_hbm.at[part], out_sems.at[j]))
        saves[-1].start()
    loads[3].wait()
    put(wop_ref, wo[...].astype(F32), 0)
    saves.append(pltpu.make_async_copy(wop_ref, wop_hbm, out_sems.at[3]))
    saves[-1].start()
    wait_all(saves)


def prepare(weight_qkv, weight_out):
    width = weight_out.shape[0]
    return pl.pallas_call(
        prepare_kernel,
        out_shape=(pltpu.HBM((3 * HEADS * HP, width), BF16), pltpu.HBM((HEADS * HP, width), BF16)),
        in_specs=[ANYWHERE] * 2,
        out_specs=(ANYWHERE, ANYWHERE),
        scratch_shapes=[
            pltpu.VMEM((3 * HEADS * HP, width), BF16),
            pltpu.VMEM((HEADS * HP, width), BF16),
            pltpu.SemaphoreType.DMA((4,)),
            pltpu.VMEM((3, width, width), BF16),
            pltpu.VMEM((width, width), BF16),
            pltpu.SemaphoreType.DMA((4,)),
        ],
        compiler_params=pltpu.CompilerParams(vmem_limit_bytes=40 * MIB),
        name="prepare",
    )(far(weight_qkv), far(weight_out))


def assemble(dst, f, own, part_of, pieces, from_ref, sems):
    count = sems.shape[1]
    part = own.shape[1]
    copies = []
    for n in range(count):
        if pieces:
            at = from_ref[n]
            src = pieces[n - 1].at[part_of] if n else own.at[at]
        else:
            at = n
            src = own.at[n]
        copies.append(pltpu.make_async_copy(src, dst.at[pl.ds(f * count * part + at * part, part)], sems.at[f, n]))
    for copy in copies:
        copy.start()
    return copies


def forward_kernel(scale, from_ref, keep_ref, wt_hbm, wo_hbm, clips, *rest):
    pieces, (out_a, out_b, x_hbm, qkv_hbm, p_hbm, inverse) = rest[:-19], rest[-19:-13]
    nrm, att, sbuf, sems, x_ref, qkv, probs, wt, wo, total, wsem, osem, ssem = rest[-13:]
    copies = []
    for f in range(2):
        copies += assemble(x_ref, f, clips.at[f], f, pieces, from_ref, sems)
    first = HP * HEADS // GROUPS
    parts = [pl.ds(j * HEADS * HP, first) for j in range(3)]
    parts += [pl.ds(j * HEADS * HP + first, HEADS * HP - first) for j in range(3)]
    weights = copy_all([(wt_hbm.at[part], wt.at[part]) for part in parts], wsem)
    out_weight = copy_all([(wo_hbm, wo)], osem)
    wait_all(copies)
    toks = x_ref.shape[0]
    frames = toks // 256
    per = HEADS // GROUPS
    rows = HP * per
    third = HEADS * HP
    x = x_ref[...].astype(F32)
    mean = jnp.mean(x, axis=-1, keepdims=True)
    centered = x - mean
    var = jnp.mean(centered * centered, axis=-1, keepdims=True)
    nrm[...] = (centered * lax.rsqrt(var + EPS)).astype(BF16)
    units = [(h, f) for h in range(HEADS) for f in range(frames)]

    def project(g):
        for j in range(3):
            part = pl.ds(j * third + g * rows, rows)
            qkv[part, :] = dot_nt(wt[part, :], nrm[...]).astype(BF16)

    def scores(i):
        h, f = units[i]
        cols = pl.ds(f * 256, 256)
        q = qkv[pl.ds(HP * h, HP), cols]
        k = qkv[pl.ds(third + HP * h, HP), cols]
        sbuf[i % 2] = dot_tn(k, q)

    def soften(i):
        h, f = units[i]
        s = sbuf[i % 2]
        top = jnp.max(s, axis=0, keepdims=True)
        e = jnp.exp2((s - top) * (scale * LOG2E))
        probs[h, :, pl.ds(f * 256, 256)] = e.astype(BF16)
        inv = 1.0 / jnp.sum(e, axis=0, keepdims=True)
        inverse[h, :, pl.ds(f * 256, 256)] = inv

    def mix(i):
        h, f = units[i]
        cols = pl.ds(f * 256, 256)
        v = qkv[pl.ds(2 * third + HP * h, HP), cols]
        att[pl.ds(HP * h, HP), cols] = (dot_nn(v, probs[h, :, cols]) * inverse[h, :, cols]).astype(BF16)

    wait_all(weights[:3])
    project(0)
    wait_all(weights[3:])
    scores(0)
    for i in range(len(units)):
        h, f = units[i]
        if f == 0 and h % per == per - 2 and h // per + 1 < GROUPS:
            project(h // per + 1)
        if f == 0 and h == HEADS // 2 + 1:
            half = pl.ds(0, HEADS // 2)
            saves = [pltpu.make_async_copy(probs.at[half], p_hbm.at[half], ssem.at[0])]
            saves[-1].start()
        if f == 0 and h == HEADS - per:
            saves += [
                pltpu.make_async_copy(qkv, qkv_hbm, ssem.at[1]),
                pltpu.make_async_copy(x_ref, x_hbm, ssem.at[2]),
            ]
            saves[-1].start()
            saves[-2].start()
        if i + 1 < len(units):
            scores(i + 1)
        soften(i)
        if i:
            mix(i - 1)
    mix(len(units) - 1)
    half = pl.ds(HEADS // 2, HEADS // 2)
    saves.append(pltpu.make_async_copy(probs.at[half], p_hbm.at[half], ssem.at[3]))
    saves[-1].start()
    wait_all(out_weight)
    projected = dot_tn(att[...], wo[...])
    total[...] = (x_ref[...].astype(F32) + projected).astype(BF16)
    for f, out_ref in enumerate((out_a, out_b)):
        part = pl.ds(f * 256, 256)

        @pl.when(keep_ref[f] == 0)
        def _():
            total[part] = jnp.zeros((256, total.shape[1]), BF16)

        saves.append(pltpu.make_async_copy(total.at[part], out_ref, ssem.at[4 + f]))
        saves[-1].start()
    wait_all(saves)


def forward(clips, pieces, origins, keep, wt, wo, scale):
    frames, part, width = clips.shape[1:]
    toks = frames * part
    out = pltpu.HBM((toks, width), BF16)
    return pl.pallas_call(
        functools.partial(forward_kernel, scale),
        out_shape=(
            out,
            out,
            pltpu.HBM((2 * toks, width), BF16),
            pltpu.HBM((wt.shape[0], 2 * toks), BF16),
            pltpu.HBM((HEADS, toks, 2 * toks), BF16),
            jax.ShapeDtypeStruct((HEADS, 1, 2 * toks), F32),
        ),
        in_specs=[IN_SMEM] * 2 + [ANYWHERE] * (3 + len(pieces)),
        out_specs=(ANYWHERE,) * 5 + (IN_VMEM,),
        scratch_shapes=[
            pltpu.VMEM((2 * toks, width), BF16),
            pltpu.VMEM((wo.shape[0], 2 * toks), BF16),
            pltpu.VMEM((2, toks, toks), F32),
            pltpu.SemaphoreType.DMA((2, frames)),
            pltpu.VMEM((2 * toks, width), BF16),
            pltpu.VMEM((wt.shape[0], 2 * toks), BF16),
            pltpu.VMEM((HEADS, toks, 2 * toks), BF16),
            pltpu.VMEM(wt.shape, BF16),
            pltpu.VMEM(wo.shape, BF16),
            pltpu.VMEM((2 * toks, width), BF16),
            pltpu.SemaphoreType.DMA((6,)),
            pltpu.SemaphoreType.DMA((1,)),
            pltpu.SemaphoreType.DMA((6,)),
        ],
        compiler_params=pltpu.CompilerParams(vmem_limit_bytes=48 * MIB),
        cost_estimate=cost(4 * toks * (wt.size + wo.size) + 8 * wo.shape[0] * toks * toks, 2 * (wt.size + wo.size)),
        name="forward",
    )(origins, keep, far(wt), far(wo), far(clips), *[far(x) for x in pieces])


def backward_kernel(scale, from_ref, keep_ref, inverse, wt_hbm, wo_hbm, x_hbm, qkv_hbm, p_hbm, cot_a, cot_b, *rest):
    pieces, (ga_ref, gb_ref, c_ref, gatt, gqkv, gabuf, gpbuf, gsbuf, sems) = rest[:-16], rest[-16:-7]
    x_ref, qkv, probs, wt, wo, total, lsem = rest[-7:]
    copies = assemble(c_ref, 0, cot_a, 2, pieces, from_ref, sems) + assemble(c_ref, 1, cot_b, 0, [], from_ref, sems)
    low, high = pl.ds(0, HEADS // 2), pl.ds(HEADS // 2, HEADS // 2)
    pairs = [(wo_hbm, wo), (qkv_hbm, qkv), (p_hbm.at[low], probs.at[low]), (p_hbm.at[high], probs.at[high])]
    loads = copy_all(pairs + [(x_hbm, x_ref), (wt_hbm, wt)], lsem)
    wait_all(copies)
    for f in range(2):
        part = c_ref[pl.ds(f * 256, 256)]
        c_ref[pl.ds(f * 256, 256)] = jnp.where(keep_ref[f] > 0, part, jnp.zeros_like(part))
    toks = x_ref.shape[0]
    frames = toks // 256
    third = HEADS * HP
    wait_all(loads[:1])
    gatt[...] = dot_nt(wo[...], c_ref[...])
    wait_all(loads[1:3])
    units = [(h, f) for h in range(HEADS) for f in range(frames)]

    def rows_of(h):
        return [pl.ds(j * third + HP * h, HP) for j in range(3)]

    def reach(i):
        h, f = units[i]
        cols = pl.ds(f * 256, 256)
        part = pl.ds(HP * h, HP)
        ga = (gatt[part, cols] * inverse[h, :, cols]).astype(BF16)
        gabuf[i % 2] = ga
        gpbuf[i % 2] = dot_tn(qkv[rows_of(h)[2], cols], ga)

    def soften(i):
        h, f = units[i]
        cols = pl.ds(f * 256, 256)
        gp = gpbuf[i % 2]
        e = probs[h, :, cols].astype(F32)
        mass = jnp.sum(e * gp, axis=0, keepdims=True) * inverse[h, :, cols]
        gsbuf[i % 2] = (e * (gp - mass) * scale).astype(BF16)

    def spread(i):
        h, f = units[i]
        cols = pl.ds(f * 256, 256)
        at = rows_of(h)
        gs = gsbuf[i % 2]
        gqkv[at[0], cols] = dot_nn(qkv[at[1], cols], gs).astype(BF16)
        gqkv[at[1], cols] = dot_nt(qkv[at[0], cols], gs).astype(BF16)

    def values(i):
        h, f = units[i]
        cols = pl.ds(f * 256, 256)
        gqkv[rows_of(h)[2], cols] = dot_nt(gabuf[i % 2], probs[h, :, cols]).astype(BF16)

    reach(0)
    for i in range(len(units)):
        if units[i] == (HEADS // 2, 0):
            wait_all(loads[3:4])
        values(i)
        if i + 1 < len(units):
            reach(i + 1)
        soften(i)
        if i:
            spread(i - 1)
    spread(len(units) - 1)
    wait_all(loads[4:])
    gn = dot_tn(gqkv[...], wt[...])
    x = x_ref[...].astype(F32)
    mean = jnp.mean(x, axis=-1, keepdims=True)
    centered = x - mean
    var = jnp.mean(centered * centered, axis=-1, keepdims=True)
    inv = lax.rsqrt(var + EPS)
    n = centered * inv
    gx = inv * (gn - jnp.mean(gn, axis=-1, keepdims=True) - n * jnp.mean(gn * n, axis=-1, keepdims=True))
    total[...] = (c_ref[...].astype(F32) + gx).astype(BF16)
    wait_all(copy_all([(total.at[pl.ds(0, 256)], ga_ref), (total.at[pl.ds(256, 256)], gb_ref)], lsem))


def backward(cot_a, cot_b, pieces, origins, keep, wt, wo, kept, scale):
    frames, part, width = cot_a.shape
    toks = frames * part
    x, qkv, probs, inverse = kept
    out = pltpu.HBM((toks, width), BF16)
    return pl.pallas_call(
        functools.partial(backward_kernel, scale),
        out_shape=(out, out),
        in_specs=[IN_SMEM] * 2 + [IN_VMEM] + [ANYWHERE] * (7 + len(pieces)),
        out_specs=(ANYWHERE, ANYWHERE),
        scratch_shapes=[
            pltpu.VMEM((2 * toks, width), BF16),
            pltpu.VMEM((wo.shape[0], 2 * toks), F32),
            pltpu.VMEM(qkv.shape, BF16),
            pltpu.VMEM((2, HP, toks), BF16),
            pltpu.VMEM((2, toks, toks), F32),
            pltpu.VMEM((2, toks, toks), BF16),
            pltpu.SemaphoreType.DMA((2, frames)),
            pltpu.VMEM(x.shape, BF16),
            pltpu.VMEM(qkv.shape, BF16),
            pltpu.VMEM(probs.shape, BF16),
            pltpu.VMEM(wt.shape, BF16),
            pltpu.VMEM(wo.shape, BF16),
            pltpu.VMEM(x.shape, BF16),
            pltpu.SemaphoreType.DMA((6,)),
        ],
        compiler_params=pltpu.CompilerParams(vmem_limit_bytes=48 * MIB),
        cost_estimate=cost(4 * toks * (wt.size + wo.size) + 16 * wo.shape[0] * toks * toks, 2 * (wt.size + wo.size)),
        name="backward",
    )(origins, keep, inverse, *[far(x) for x in (wt, wo, x, qkv, probs, cot_a, cot_b)], *[far(x) for x in pieces])


def shuffle_kernel(index_ref, x_ref, out_ref):
    for i in range(x_ref.shape[0]):
        out_ref[i] = x_ref[index_ref[i]]


def shuffle(x, index):
    return pl.pallas_call(
        shuffle_kernel,
        out_shape=jax.ShapeDtypeStruct(x.shape, x.dtype),
        in_specs=[IN_SMEM, IN_VMEM],
        out_specs=IN_VMEM,
        compiler_params=pltpu.CompilerParams(vmem_limit_bytes=8 * MIB),
        name="shuffle",
    )(index, x)


def spread(x, groups):
    return lax.all_to_all(x.reshape(groups, -1, x.shape[-1]), "grp", 0, 0, tiled=True)


def pack_kernel(leads, to_ref, *refs):
    count = len(leads)
    sources, outs, sems = refs[:count], refs[count:-1], refs[-1]
    copies = []
    for n, out in enumerate(outs):
        at = to_ref[n + 1]
        for a, lead in enumerate(leads):
            src = sources[a] if lead is None else sources[a].at[lead[0]]
            copies.append(pltpu.make_async_copy(src.at[at], out.at[a], sems.at[n, a]))
    for copy in copies:
        copy.start()
    for copy in copies:
        copy.wait()


def pack(sources, leads, targets):
    n = targets.shape[0]
    block = sources[0].shape[-2:]
    return pl.pallas_call(
        functools.partial(pack_kernel, leads),
        out_shape=(jax.ShapeDtypeStruct((len(leads),) + block, BF16),) * (n - 1),
        in_specs=[IN_SMEM] + [ANYWHERE] * len(sources),
        out_specs=(IN_VMEM,) * (n - 1),
        scratch_shapes=[pltpu.SemaphoreType.DMA((n - 1, len(leads)))],
        compiler_params=pltpu.CompilerParams(vmem_limit_bytes=12 * MIB),
        name="pack",
    )(targets, *[far(x) for x in sources])


def unpack_kernel(picks, from_ref, *refs):
    owns = len(picks)
    sources, (out, held, in_sems, out_sems) = refs[:-4], refs[-4:]
    own, pieces = sources[:owns], sources[owns:]
    reads, writes = [], []
    for a, pick in enumerate(picks):
        for n in range(in_sems.shape[1]):
            at = from_ref[n]
            first, clip = pick
            src = pieces[first + n - 1].at[clip] if n else own[a].at[at]
            reads.append(pltpu.make_async_copy(src, held.at[a, n], in_sems.at[a, n]))
            writes.append(pltpu.make_async_copy(held.at[a, n], out.at[a, at], out_sems.at[a, n]))
    for read in reads:
        read.start()
    for read, write in zip(reads, writes):
        read.wait()
        write.start()
    wait_all(writes)


def unpack(own, pieces, picks, origins):
    n = origins.shape[0]
    shape = (len(picks),) + own[0].shape
    return pl.pallas_call(
        functools.partial(unpack_kernel, picks),
        out_shape=pltpu.HBM(shape, BF16),
        in_specs=[IN_SMEM] + [ANYWHERE] * (len(own) + len(pieces)),
        out_specs=ANYWHERE,
        scratch_shapes=[
            pltpu.VMEM(shape, BF16),
            pltpu.SemaphoreType.DMA((len(picks), n)),
            pltpu.SemaphoreType.DMA((len(picks), n)),
        ],
        compiler_params=pltpu.CompilerParams(vmem_limit_bytes=12 * MIB),
        name="unpack",
    )(origins, *[far(x) for x in own], *[far(x) for x in pieces])


def exchange(sends, size):
    chips = size // 2
    out = []
    for n, x in enumerate(sends, start=1):
        pairs = [(i, (i // 2 + n // 2) % chips * 2 + (i % 2 ^ n % 2)) for i in range(size)]
        out.append(lax.ppermute(x, "sp", pairs))
    return out


def settle(pieces, *others):
    across = [n for n in range(len(pieces)) if (n + 1) // 2 == (len(pieces) + 1) // 4]
    near = [n for n in range(len(pieces)) if n not in across]
    *held, rest = lax.optimization_barrier((*[pieces[n] for n in near], others))
    pieces = list(pieces)
    for n, piece in zip(near, held):
        pieces[n] = piece
    return (pieces, *rest)


def on_device(clips, counts, dest, weight_qkv, weight_out, cotangent):
    groups = lax.axis_size("grp")
    size = lax.axis_size("sp")
    me = lax.axis_index("grp")
    frame = lax.axis_index("sp")
    order = jnp.arange(groups, dtype=jnp.int32)
    source = jnp.sum(jnp.where(dest[None, :] == order[:, None], order[None, :], 0), axis=1)
    offset = jnp.arange(size, dtype=jnp.int32)
    targets = (frame // 2 + offset // 2) % (size // 2) * 2 + (frame + offset) % 2
    origins = (frame // 2 - offset // 2) % (size // 2) * 2 + (frame + offset) % 2
    scale = (weight_out.shape[0] // HEADS) ** -0.5
    used = lax.dynamic_slice_in_dim(counts, 2 * me, 2)
    keep = (frame < used).astype(jnp.int32)
    keep_a, keep_b = keep[0:1], keep[1:2]

    block = clips.shape[1:]
    cot_b = spread(cotangent[1], groups)
    pieces = exchange(pack((clips, clips, cotangent), ((0,), (1,), (0,)), targets), size)
    wt, wo = prepare(weight_qkv, weight_out)
    pieces, cot_b, wt = settle(pieces, cot_b, wt)
    cot_b = spread(shuffle(cot_b, dest), groups).reshape(block)
    cot_b, wt = lax.optimization_barrier((cot_b, wt))
    out_a, out_b, *kept = forward(clips, pieces, origins, keep, wt, wo, scale)
    cot_b = lax.all_to_all(cot_b, "sp", 0, 0, tiled=True)
    cot_b, out_b = lax.optimization_barrier((cot_b, out_b))
    out_b = spread(out_b, groups)
    grad_a, grad_b = backward(cotangent[0], cot_b, pieces, origins, keep, wt, wo, kept, scale)
    grad_a, grad_b, out_a = grad_a.reshape(block), grad_b.reshape(block), out_a.reshape(block)
    sends = pack((grad_a, grad_b, out_a), (None, None, None), targets)
    out_b, sends = lax.optimization_barrier((out_b, sends))
    back = exchange(sends, size)
    out_b = spread(shuffle(out_b, source), groups).reshape(block)
    back, out_b = settle(back, out_b)
    late = exchange(pack((out_b,), (None,), targets), size)
    grads = unpack((grad_a, grad_b), back, ((0, 0), (0, 1)), origins)
    outputs = unpack((out_a, out_b), back + late, ((0, 2), (len(back), 0)), origins)
    return (outputs, grads)


def solution(mesh):
    spec = P("grp", None, "sp", None)
    return jax.shard_map(
        on_device, mesh=mesh, in_specs=(spec, P(), P(), P(), P(), spec), out_specs=(spec, spec), check_vma=False
    )
```

time: 613 us -> 153 us (0.25); the launches traced: 603 us -> 152 us
  waiting for transfers between devices: 366 us -> 17.7 us
  local copies, waits for them, and re-layouts: 115 us -> 4.65 us
  Pallas kernels: 0 us -> 59.5 us
  matrix products: 52.7 us -> 0 us
  starting transfers between devices: 36.5 us -> 68.5 us
  other arithmetic: 27.6 us -> 0.22 us
    all_to_all x6 -> x5, waiting for transfers between devices: 366 us -> 7.84 us  [the longest x4 7.83 us: spread(): lax.all_to_all(x.reshape(groups, -1, x.shape[-1]), 'grp', 0, 0, tiled=True)]
    pallas_call x0 -> x10, Pallas kernels: none -> 59.5 us  [the longest x1 21 us: backward(): pl.pallas_call(functools.partial(backward_kernel, scale), out_shape=(out,...]
    reshape x6 -> x0, local copies, waits for them, and re-layouts: 56 us -> none  [the longest x2 20.7 us: on_device(): qkv = qkv.reshape(work.shape[:-1] + (3, HEADS, head_dim))]
    dot_general x10 -> x0, matrix products: 52.7 us -> none  [the longest x3 14.5 us: attend(): jnp.einsum('...hqk,...khe->...qhe', probs, values, preferred_element_type...]
    ppermute x0 -> x21, starting transfers between devices: none -> 38.4 us  [exchange(): out.append(lax.ppermute(x, 'sp', pairs))]
    all_to_all x7 -> x0, local copies, waits for them, and re-layouts: 28.9 us -> none  [the longest x2 11.3 us: on_device(): lax.all_to_all(grad_qkv, 'sp', split_axis=2, concat_axis=4, tiled=True)]
    another operation x1 -> x0, local copies, waits for them, and re-layouts: 15.9 us -> none  [on_device(): grad_qkv = jnp.stack([grad_q, grad_k, grad_v], axis=-3)]
    reduce_sum x6 -> x1, other arithmetic: 10.5 us -> 0.11 us  [on_device(): jnp.sum(jnp.where(dest[None, :] == order[:, None], order[None, :], 0), ax...]
  transfers between devices with their start and end apart: 6 -> 26, of which waited for: 4 -> 8; matrix products, arithmetic and copies ran while one was open for 22% -> 0% of each run, Pallas kernels for 0% -> 36%
where the time goes in v2:
time: 153 us; the launch traced here: 152 us
  starting transfers between devices  68.5 us (45%)
  Pallas kernels  59.5 us (39%)
  waiting for transfers between devices  17.7 us (12%)
  local copies, waits for them, and re-layouts  4.65 us (3%)
    ppermute x21, starting transfers between devices, exchange(): out.append(lax.ppermute(x, 'sp', pairs))  38.4 us
    all_to_all x4, starting transfers between devices, spread(): lax.all_to_all(x.reshape(groups, -1, x.shape[-1]), 'grp', 0, 0, tiled=True)  24.7 us
    pallas_call x1, Pallas kernels, backward(): pl.pallas_call(functools.partial(backward_kernel, scale), out_shape=(out,...  21 us
    pallas_call x1, Pallas kernels, forward(): pl.pallas_call(functools.partial(forward_kernel, scale), out_shape=(out,...  16.7 us
    ppermute x21, waiting for transfers between devices, exchange(): out.append(lax.ppermute(x, 'sp', pairs))  9.83 us
    all_to_all x4, waiting for transfers between devices, spread(): lax.all_to_all(x.reshape(groups, -1, x.shape[-1]), 'grp', 0, 0, tiled=True)  7.83 us
    pallas_call x1, Pallas kernels, prepare(): pl.pallas_call(prepare_kernel, out_shape=(pltpu.HBM((3 * HEADS * HP, widt...  7.34 us
    pallas_call x3, Pallas kernels, pack(): pl.pallas_call(functools.partial(pack_kernel, leads), out_shape=(jax.Shap...  6.06 us
  transfers between devices with their start and end apart: 26, of which 8 were waited for; matrix products, arithmetic and copies ran while one was open for 0% of the time, Pallas kernels for 36%

profile of v2, /device:TPU:1, one launch (start us, length us, event | category | flops | bytes accessed | tf_op | source)
XLA Modules:
  0.0 151.7 jit_solution(4479688755834920476)
XLA Ops:
  0.6 2.3 %slice_bitcast_fusion = (bf16[8,32,1152]{2,1,0:T(8,128)(2,1)}, bf16[1,8,32,1152]{3,2,1,0:T(8,128)(2,1)}) fusion(bf16[2,8,32,1152]{3,2,1,0:T(8,128)(2,1)} %refs_2_.1), kind=kLoop, calls=%fused_computation | loop fusion | bytes 2359296 | tf_op jit(solution)/shard_map/squeeze | solution.py:491
  3.0 7.6 %all-to-all-start = ((bf16[16,16,1152]{2,1,0:T(8,128)(2,1)}), bf16[16,16,1152]{2,1,0:T(8,128)(2,1)S(1)}, u32[]{:S(2)}, u32[]{:S(2)}) async-start(bf16[16,16,1152]{2,1,0:T(8,128)(2,1)} %bitcast), calls=%async_computation | async-start | bytes 1179648 | tf_op jit(solution)/shard_map/all_to_all | solution.py:376
  10.6 2.2 %pack.3 = (bf16[3,32,1152]{2,1,0:T(8,128)(2,1)S(1)}, bf16[3,32,1152]{2,1,0:T(8,128)(2,1)S(1)}, bf16[3,32,1152]{2,1,0:T(8,128)(2,1)S(1)}, bf16[3,32,1152]{2,1,0:T...) custom-call(s32[8]{0:T(128)S(1)} %fusion.3.to_ref, ...), custom_call_target="tpu_custom_call" | custom-call | tf_op jit(solution)/shard_map/pack/pallas_call | solution.py:397
  15.5 1.9 %collective-permute-start.2 = (bf16[3,32,1152]{2,1,0:T(8,128)(2,1)S(1)}, bf16[3,32,1152]{2,1,0:T(8,128)(2,1)S(1)}, u32[]{:S(2)}, u32[]{:S(2)}) collective-permute-start(bf16[3,32,1152]{2,1,0:T(8,128)(2,1)S(1)} %get-tuple-element.60), channel_id=1, source_target_pairs={{0,3},{1,2},{2,5},{3,4},{4,7},{5,6},{6,1},{7,0},{8,11},{9,10},{10,... | collective-permute-start | bytes 663560 | tf_op jit(solution)/shard_map/ppermute | solution.py:451
  19.6 7.3 %prepare.1 = (bf16[3840,1152]{1,0:T(8,128)(2,1)}, bf16[1280,1152]{1,0:T(8,128)(2,1)}) custom-call(bf16[1152,3456]{1,0:T(8,128)(2,1)} %wq_hbm.1, bf16[1152,1152]{1,0:T(8,128)(2,1)} %wo_hbm.1), custom_call_target="tpu_custom_call" | custom-call | tf_op jit(solution)/shard_map/prepare/pallas_call | solution.py:86
  30.7 7.0 %all-to-all-start.1 = ((bf16[16,16,1152]{2,1,0:T(8,128)(2,1)}), bf16[16,16,1152]{2,1,0:T(8,128)(2,1)}, u32[]{:S(2)}, u32[]{:S(2)}) async-start(bf16[16,16,1152]{2,1,0:T(8,128)(2,1)} %shuffle.2), calls=%async_computation.1 | async-start | bytes 1179648 | tf_op jit(solution)/shard_map/all_to_all | solution.py:376
  39.2 2.1 %collective-permute-start.6 = (bf16[3,32,1152]{2,1,0:T(8,128)(2,1)S(1)}, bf16[3,32,1152]{2,1,0:T(8,128)(2,1)S(1)}, u32[]{:S(2)}, u32[]{:S(2)}) collective-permute-start(bf16[3,32,1152]{2,1,0:T(8,128)(2,1)S(1)} %get-tuple-element.72), channel_id=1, source_target_pairs={{0,5},{1,4},{2,7},{3,6},{4,1},{5,0},{6,3},{7,2},{8,13},{9,12},{10,... | collective-permute-start | bytes 663560 | tf_op jit(solution)/shard_map/ppermute | solution.py:451
  41.5 7.8 %all-to-all-done.1 = bf16[16,16,1152]{2,1,0:T(8,128)(2,1)} async-done(((bf16[16,16,1152]{2,1,0:T(8,128)(2,1)}), bf16[16,16,1152]{2,1,0:T(8,128)(2,1)}, u32[]{:S(2)}, u32[]{:S(2)}) %all-to-all-start.1) | async-done | bytes 589856 | tf_op jit(solution)/shard_map/all_to_all | solution.py:376
  49.3 5.4 %all-to-all-start.2 = ((bf16[8,32,1152]{2,1,0:T(8,128)(2,1)}), bf16[8,32,1152]{2,1,0:T(8,128)(2,1)S(1)}, u32[]{:S(2)}, u32[]{:S(2)}) async-start(bf16[8,32,1152]{2,1,0:T(8,128)(2,1)} %bitcast.1), calls=%async_computation.2 | async-start | bytes 1179648 | tf_op jit(solution)/shard_map/all_to_all | solution.py:488
  55.5 16.7 %forward.1 = (bf16[256,1152]{1,0:T(8,128)(2,1)}, bf16[256,1152]{1,0:T(8,128)(2,1)}, bf16[512,1152]{1,0:T(8,128)(2,1)}, bf16[3840,512]{1,0:T(8,128)(2,1)}, bf16[1...) custom-call(s32[8]{0:T(128)S(1)} %fusion.1.from_ref, s32[2]{0:T(128)S(1)} %compare_convert_fusion.keep_ref, ...), custom_call_target="tpu_custom_call" | custom-call | flops 6710886400 | bytes 11796480 | tf_op jit(solution)/shard_map/forward/pallas_call | solution.py:219
  72.2 3.8 %all-to-all-start.3 = ((bf16[16,16,1152]{2,1,0:T(8,128)(2,1)}), bf16[16,16,1152]{2,1,0:T(8,128)(2,1)S(1)}, u32[]{:S(2)}, u32[]{:S(2)}) async-start(bf16[16,16,1152]{2,1,0:T(8,128)(2,1)} %bitcast.17), calls=%async_computation.3 | async-start | bytes 1179648 | tf_op jit(solution)/shard_map/all_to_all | solution.py:376
  76.0 21.0 %backward.1 = (bf16[256,1152]{1,0:T(8,128)(2,1)}, bf16[256,1152]{1,0:T(8,128)(2,1)}) custom-call(s32[8]{0:T(128)S(1)} %fusion.1.from_ref, s32[2]{0:T(128)S(1)} %compare_convert_fusion.keep_ref, f32[16,1,512]{2,1,0:T(1,128)S(1)} %get-tuple-element.79.inverse, bf16[3840,1152]{1,0:T(8,128)(2,1)} %get-tuple-element.66.wt_hbm, ...), custom_call_target="tpu_custom_call" | custom-call | flops 7381975040 | bytes 11796480 | tf_op jit(solution)/shard_map/backward/pallas_call | solution.py:332
  97.1 2.2 %pack.4 = (bf16[3,32,1152]{2,1,0:T(8,128)(2,1)S(1)}, bf16[3,32,1152]{2,1,0:T(8,128)(2,1)S(1)}, bf16[3,32,1152]{2,1,0:T(8,128)(2,1)S(1)}, bf16[3,32,1152]{2,1,0:T...) custom-call(s32[8]{0:T(128)S(1)} %fusion.3.to_ref, ...), custom_call_target="tpu_custom_call" | custom-call | tf_op jit(solution)/shard_map/pack/pallas_call | solution.py:397
  100.7 6.4 %all-to-all-start.4 = ((bf16[16,16,1152]{2,1,0:T(8,128)(2,1)}), bf16[16,16,1152]{2,1,0:T(8,128)(2,1)S(1)}, u32[]{:S(2)}, u32[]{:S(2)}) async-start(bf16[16,16,1152]{2,1,0:T(8,128)(2,1)} %shuffle.3), calls=%async_computation.4 | async-start | bytes 1179648 | tf_op jit(solution)/shard_map/all_to_all | solution.py:376
  107.7 1.8 %collective-permute-start.8 = (bf16[3,32,1152]{2,1,0:T(8,128)(2,1)S(1)}, bf16[3,32,1152]{2,1,0:T(8,128)(2,1)S(1)}, u32[]{:S(2)}, u32[]{:S(2)}) collective-permute-start(bf16[3,32,1152]{2,1,0:T(8,128)(2,1)S(1)} %get-tuple-element.94), channel_id=1, source_target_pairs={{0,2},{1,3},{2,4},{3,5},{4,6},{5,7},{6,0},{7,1},{8,10},{9,11},{10,... | collective-permute-start | bytes 663560 | tf_op jit(solution)/shard_map/ppermute | solution.py:451
  109.5 1.7 %collective-permute-start.9 = (bf16[3,32,1152]{2,1,0:T(8,128)(2,1)S(1)}, bf16[3,32,1152]{2,1,0:T(8,128)(2,1)S(1)}, u32[]{:S(2)}, u32[]{:S(2)}) collective-permute-start(bf16[3,32,1152]{2,1,0:T(8,128)(2,1)S(1)} %get-tuple-element.95), channel_id=1, source_target_pairs={{0,3},{1,2},{2,5},{3,4},{4,7},{5,6},{6,1},{7,0},{8,11},{9,10},{10,... | collective-permute-start | bytes 663560 | tf_op jit(solution)/shard_map/ppermute | solution.py:451
  114.5 1.7 %collective-permute-done.8.refs_3_ = bf16[3,32,1152]{2,1,0:T(8,128)(2,1)S(1)} collective-permute-done((bf16[3,32,1152]{2,1,0:T(8,128)(2,1)S(1)}, bf16[3,32,1152]{2,1,0:T(8,128)(2,1)S(1)}, u32[]{:S(2)}, u32[]{:S(2)}) %collective-permute-start.8) | collective-permute-done | bytes 221216 | tf_op jit(solution)/shard_map/ppermute | solution.py:451
  116.2 3.3 %collective-permute-start.13 = (bf16[3,32,1152]{2,1,0:T(8,128)(2,1)S(1)}, bf16[3,32,1152]{2,1,0:T(8,128)(2,1)S(1)}, u32[]{:S(2)}, u32[]{:S(2)}) collective-permute-start(bf16[3,32,1152]{2,1,0:T(8,128)(2,1)S(1)} %get-tuple-element.104), channel_id=1, source_target_pairs={{0,5},{1,4},{2,7},{3,6},{4,1},{5,0},{6,3},{7,2},{8,13},{9,12},{10,... | collective-permute-start | bytes 663560 | tf_op jit(solution)/shard_map/ppermute | solution.py:451
  121.2 2.5 %collective-permute-done.11.refs_8_ = bf16[3,32,1152]{2,1,0:T(8,128)(2,1)S(1)} collective-permute-done((bf16[3,32,1152]{2,1,0:T(8,128)(2,1)S(1)}, bf16[3,32,1152]{2,1,0:T(8,128)(2,1)S(1)}, u32[]{:S(2)}, u32[]{:S(2)}) %collective-permute-start.11) | collective-permute-done | bytes 221216 | tf_op jit(solution)/shard_map/ppermute | solution.py:451
  126.2 9.0 %collective-permute-start.14 = (bf16[1,32,1152]{2,1,0:T(8,128)(2,1)S(1)}, bf16[1,32,1152]{2,1,0:T(8,128)(2,1)S(1)}, u32[]{:S(2)}, u32[]{:S(2)}) collective-permute-start(bf16[1,32,1152]{2,1,0:T(8,128)(2,1)S(1)} %get-tuple-element.107), channel_id=1, source_target_pairs={{0,1},{1,0},{2,3},{3,2},{4,5},{5,4},{6,7},{7,6},{8,9},{9,8},{10,11... | collective-permute-start | bytes 221192 | tf_op jit(solution)/shard_map/ppermute | solution.py:451
  136.5 3.0 %collective-permute-start.17 = (bf16[1,32,1152]{2,1,0:T(8,128)(2,1)S(1)}, bf16[1,32,1152]{2,1,0:T(8,128)(2,1)S(1)}, u32[]{:S(2)}, u32[]{:S(2)}) collective-permute-start(bf16[1,32,1152]{2,1,0:T(8,128)(2,1)S(1)} %get-tuple-element.110), channel_id=1, source_target_pairs={{0,4},{1,5},{2,6},{3,7},{4,0},{5,1},{6,2},{7,3},{8,12},{9,13},{10,... | collective-permute-start | bytes 221192 | tf_op jit(solution)/shard_map/ppermute | solution.py:451
  140.1 2.3 %collective-permute-start.19 = (bf16[1,32,1152]{2,1,0:T(8,128)(2,1)S(1)}, bf16[1,32,1152]{2,1,0:T(8,128)(2,1)S(1)}, u32[]{:S(2)}, u32[]{:S(2)}) collective-permute-start(bf16[1,32,1152]{2,1,0:T(8,128)(2,1)S(1)} %get-tuple-element.112), channel_id=1, source_target_pairs={{0,6},{1,7},{2,0},{3,1},{4,2},{5,3},{6,4},{7,5},{8,14},{9,15},{10,... | collective-permute-start | bytes 221192 | tf_op jit(solution)/shard_map/ppermute | solution.py:451
  143.5 2.8 %unpack.3 = bf16[2,8,32,1152]{3,2,1,0:T(8,128)(2,1)} custom-call(s32[8]{0:T(128)S(1)} %fusion.1.from_ref, bf16[8,32,1152]{2,1,0:T(8,128)(2,1)} %bitcast.14, bf16[8,32,1152]{2,1,0:T(8,128)(2,1)} %bitcast.16, bf16[3,32,1152]{2,1,0:T(8,128)(2,1)} %copy-done.2, bf16[3,32,1152]{2,1,0:T(8,128)(2,1)} %copy-done.3, bf16[3,32,1152]{2,1,0:T(8,128)(2,1)} %copy-done.4, ...), custom_call_target="tpu_custom_call" | custom-call | tf_op jit(solution)/shard_map/unpack/pallas_call | solution.py:431
  148.7 2.8 %unpack.2 = bf16[2,8,32,1152]{3,2,1,0:T(8,128)(2,1)} custom-call(s32[8]{0:T(128)S(1)} %fusion.1.from_ref, bf16[8,32,1152]{2,1,0:T(8,128)(2,1)} %bitcast.12, bf16[8,32,1152]{2,1,0:T(8,128)(2,1)} %bitcast.10, bf16[3,32,1152]{2,1,0:T(8,128)(2,1)} %copy-done.2, bf16[3,32,1152]{2,1,0:T(8,128)(2,1)} %copy-done.3, bf16[3,32,1152]{2,1,0:T(8,128)(2,1)} %copy-done.4, ...), custom_call_target="tpu_custom_call" | custom-call | tf_op jit(solution)/shard_map/unpack/pallas_call | solution.py:431
  (93 shorter events, 26.1 us)
Async XLA Ops:
  3.0 26.3 %all-to-all-start = ((bf16[16,16,1152]{2,1,0:T(8,128)(2,1)}), bf16[16,16,1152]{2,1,0:T(8,128)(2,1)S(1)}, u32[]{:S(2)}, u32[]{:S(2)}) async-start(bf16[16,16,1152]{2,1,0:T(8,128)(2,1)} %bitcast), calls=%async_computation | async-start | bytes 1179648 | tf_op jit(solution)/shard_map/all_to_all | solution.py:376
  12.8 14.2 %collective-permute-start = (bf16[3,32,1152]{2,1,0:T(8,128)(2,1)S(1)}, bf16[3,32,1152]{2,1,0:T(8,128)(2,1)S(1)}, u32[]{:S(2)}, u32[]{:S(2)}) collective-permute-start(bf16[3,32,1152]{2,1,0:T(8,128)(2,1)S(1)} %get-tuple-element.58), channel_id=1, source_target_pairs={{0,1},{1,0},{2,3},{3,2},{4,5},{5,4},{6,7},{7,6},{8,9},{9,8},{10,11... | collective-permute-start | bytes 663560 | tf_op jit(solution)/shard_map/ppermute | solution.py:451
  13.8 13.2 %collective-permute-start.1 = (bf16[3,32,1152]{2,1,0:T(8,128)(2,1)S(1)}, bf16[3,32,1152]{2,1,0:T(8,128)(2,1)S(1)}, u32[]{:S(2)}, u32[]{:S(2)}) collective-permute-start(bf16[3,32,1152]{2,1,0:T(8,128)(2,1)S(1)} %get-tuple-element.59), channel_id=1, source_target_pairs={{0,2},{1,3},{2,4},{3,5},{4,6},{5,7},{6,0},{7,1},{8,10},{9,11},{10,... | collective-permute-start | bytes 663560 | tf_op jit(solution)/shard_map/ppermute | solution.py:451
  15.5 12.6 %collective-permute-start.2 = (bf16[3,32,1152]{2,1,0:T(8,128)(2,1)S(1)}, bf16[3,32,1152]{2,1,0:T(8,128)(2,1)S(1)}, u32[]{:S(2)}, u32[]{:S(2)}) collective-permute-start(bf16[3,32,1152]{2,1,0:T(8,128)(2,1)S(1)} %get-tuple-element.60), channel_id=1, source_target_pairs={{0,3},{1,2},{2,5},{3,4},{4,7},{5,6},{6,1},{7,0},{8,11},{9,10},{10,... | collective-permute-start | bytes 663560 | tf_op jit(solution)/shard_map/ppermute | solution.py:451
  17.3 10.7 %collective-permute-start.3 = (bf16[3,32,1152]{2,1,0:T(8,128)(2,1)S(1)}, bf16[3,32,1152]{2,1,0:T(8,128)(2,1)S(1)}, u32[]{:S(2)}, u32[]{:S(2)}) collective-permute-start(bf16[3,32,1152]{2,1,0:T(8,128)(2,1)S(1)} %get-tuple-element.61), channel_id=1, source_target_pairs={{0,6},{1,7},{2,0},{3,1},{4,2},{5,3},{6,4},{7,5},{8,14},{9,15},{10,... | collective-permute-start | bytes 663560 | tf_op jit(solution)/shard_map/ppermute | solution.py:451
  18.4 10.9 %collective-permute-start.4 = (bf16[3,32,1152]{2,1,0:T(8,128)(2,1)S(1)}, bf16[3,32,1152]{2,1,0:T(8,128)(2,1)S(1)}, u32[]{:S(2)}, u32[]{:S(2)}) collective-permute-start(bf16[3,32,1152]{2,1,0:T(8,128)(2,1)S(1)} %get-tuple-element.62), channel_id=1, source_target_pairs={{0,7},{1,6},{2,1},{3,0},{4,3},{5,2},{6,5},{7,4},{8,15},{9,14},{10,... | collective-permute-start | bytes 663560 | tf_op jit(solution)/shard_map/ppermute | solution.py:451
  30.7 18.7 %all-to-all-start.1 = ((bf16[16,16,1152]{2,1,0:T(8,128)(2,1)}), bf16[16,16,1152]{2,1,0:T(8,128)(2,1)}, u32[]{:S(2)}, u32[]{:S(2)}) async-start(bf16[16,16,1152]{2,1,0:T(8,128)(2,1)} %shuffle.2), calls=%async_computation.1 | async-start | bytes 1179648 | tf_op jit(solution)/shard_map/all_to_all | solution.py:376
  37.6 17.1 %collective-permute-start.5 = (bf16[3,32,1152]{2,1,0:T(8,128)(2,1)S(1)}, bf16[3,32,1152]{2,1,0:T(8,128)(2,1)S(1)}, u32[]{:S(2)}, u32[]{:S(2)}) collective-permute-start(bf16[3,32,1152]{2,1,0:T(8,128)(2,1)S(1)} %get-tuple-element.71), channel_id=1, source_target_pairs={{0,4},{1,5},{2,6},{3,7},{4,0},{5,1},{6,2},{7,3},{8,12},{9,13},{10,... | collective-permute-start | bytes 663560 | tf_op jit(solution)/shard_map/ppermute | solution.py:451
  39.2 15.5 %collective-permute-start.6 = (bf16[3,32,1152]{2,1,0:T(8,128)(2,1)S(1)}, bf16[3,32,1152]{2,1,0:T(8,128)(2,1)S(1)}, u32[]{:S(2)}, u32[]{:S(2)}) collective-permute-start(bf16[3,32,1152]{2,1,0:T(8,128)(2,1)S(1)} %get-tuple-element.72), channel_id=1, source_target_pairs={{0,5},{1,4},{2,7},{3,6},{4,1},{5,0},{6,3},{7,2},{8,13},{9,12},{10,... | collective-permute-start | bytes 663560 | tf_op jit(solution)/shard_map/ppermute | solution.py:451
  49.3 22.9 %all-to-all-start.2 = ((bf16[8,32,1152]{2,1,0:T(8,128)(2,1)}), bf16[8,32,1152]{2,1,0:T(8,128)(2,1)S(1)}, u32[]{:S(2)}, u32[]{:S(2)}) async-start(bf16[8,32,1152]{2,1,0:T(8,128)(2,1)} %bitcast.1), calls=%async_computation.2 | async-start | bytes 1179648 | tf_op jit(solution)/shard_map/all_to_all | solution.py:488
  72.2 27.1 %all-to-all-start.3 = ((bf16[16,16,1152]{2,1,0:T(8,128)(2,1)}), bf16[16,16,1152]{2,1,0:T(8,128)(2,1)S(1)}, u32[]{:S(2)}, u32[]{:S(2)}) async-start(bf16[16,16,1152]{2,1,0:T(8,128)(2,1)} %bitcast.17), calls=%async_computation.3 | async-start | bytes 1179648 | tf_op jit(solution)/shard_map/all_to_all | solution.py:376
  100.7 22.9 %all-to-all-start.4 = ((bf16[16,16,1152]{2,1,0:T(8,128)(2,1)}), bf16[16,16,1152]{2,1,0:T(8,128)(2,1)S(1)}, u32[]{:S(2)}, u32[]{:S(2)}) async-start(bf16[16,16,1152]{2,1,0:T(8,128)(2,1)} %shuffle.3), calls=%async_computation.4 | async-start | bytes 1179648 | tf_op jit(solution)/shard_map/all_to_all | solution.py:376
  107.7 8.5 %collective-permute-start.8 = (bf16[3,32,1152]{2,1,0:T(8,128)(2,1)S(1)}, bf16[3,32,1152]{2,1,0:T(8,128)(2,1)S(1)}, u32[]{:S(2)}, u32[]{:S(2)}) collective-permute-start(bf16[3,32,1152]{2,1,0:T(8,128)(2,1)S(1)} %get-tuple-element.94), channel_id=1, source_target_pairs={{0,2},{1,3},{2,4},{3,5},{4,6},{5,7},{6,0},{7,1},{8,10},{9,11},{10,... | collective-permute-start | bytes 663560 | tf_op jit(solution)/shard_map/ppermute | solution.py:451
  109.5 11.7 %collective-permute-start.9 = (bf16[3,32,1152]{2,1,0:T(8,128)(2,1)S(1)}, bf16[3,32,1152]{2,1,0:T(8,128)(2,1)S(1)}, u32[]{:S(2)}, u32[]{:S(2)}) collective-permute-start(bf16[3,32,1152]{2,1,0:T(8,128)(2,1)S(1)} %get-tuple-element.95), channel_id=1, source_target_pairs={{0,3},{1,2},{2,5},{3,4},{4,7},{5,6},{6,1},{7,0},{8,11},{9,10},{10,... | collective-permute-start | bytes 663560 | tf_op jit(solution)/shard_map/ppermute | solution.py:451
  111.2 10.0 %collective-permute-start.10 = (bf16[3,32,1152]{2,1,0:T(8,128)(2,1)S(1)}, bf16[3,32,1152]{2,1,0:T(8,128)(2,1)S(1)}, u32[]{:S(2)}, u32[]{:S(2)}) collective-permute-start(bf16[3,32,1152]{2,1,0:T(8,128)(2,1)S(1)} %get-tuple-element.96), channel_id=1, source_target_pairs={{0,6},{1,7},{2,0},{3,1},{4,2},{5,3},{6,4},{7,5},{8,14},{9,15},{10,... | collective-permute-start | bytes 663560 | tf_op jit(solution)/shard_map/ppermute | solution.py:451
  112.7 11.0 %collective-permute-start.11 = (bf16[3,32,1152]{2,1,0:T(8,128)(2,1)S(1)}, bf16[3,32,1152]{2,1,0:T(8,128)(2,1)S(1)}, u32[]{:S(2)}, u32[]{:S(2)}) collective-permute-start(bf16[3,32,1152]{2,1,0:T(8,128)(2,1)S(1)} %get-tuple-element.97), channel_id=1, source_target_pairs={{0,7},{1,6},{2,1},{3,0},{4,3},{5,2},{6,5},{7,4},{8,15},{9,14},{10,... | collective-permute-start | bytes 663560 | tf_op jit(solution)/shard_map/ppermute | solution.py:451
  113.0 23.6 %collective-permute-start.12 = (bf16[3,32,1152]{2,1,0:T(8,128)(2,1)S(1)}, bf16[3,32,1152]{2,1,0:T(8,128)(2,1)S(1)}, u32[]{:S(2)}, u32[]{:S(2)}) collective-permute-start(bf16[3,32,1152]{2,1,0:T(8,128)(2,1)S(1)} %get-tuple-element.103), channel_id=1, source_target_pairs={{0,4},{1,5},{2,6},{3,7},{4,0},{5,1},{6,2},{7,3},{8,12},{9,13},{10,... | collective-permute-start | bytes 663560 | tf_op jit(solution)/shard_map/ppermute | solution.py:451
  116.2 23.3 %collective-permute-start.13 = (bf16[3,32,1152]{2,1,0:T(8,128)(2,1)S(1)}, bf16[3,32,1152]{2,1,0:T(8,128)(2,1)S(1)}, u32[]{:S(2)}, u32[]{:S(2)}) collective-permute-start(bf16[3,32,1152]{2,1,0:T(8,128)(2,1)S(1)} %get-tuple-element.104), channel_id=1, source_target_pairs={{0,5},{1,4},{2,7},{3,6},{4,1},{5,0},{6,3},{7,2},{8,13},{9,12},{10,... | collective-permute-start | bytes 663560 | tf_op jit(solution)/shard_map/ppermute | solution.py:451
  126.2 13.9 %collective-permute-start.14 = (bf16[1,32,1152]{2,1,0:T(8,128)(2,1)S(1)}, bf16[1,32,1152]{2,1,0:T(8,128)(2,1)S(1)}, u32[]{:S(2)}, u32[]{:S(2)}) collective-permute-start(bf16[1,32,1152]{2,1,0:T(8,128)(2,1)S(1)} %get-tuple-element.107), channel_id=1, source_target_pairs={{0,1},{1,0},{2,3},{3,2},{4,5},{5,4},{6,7},{7,6},{8,9},{9,8},{10,11... | collective-permute-start | bytes 221192 | tf_op jit(solution)/shard_map/ppermute | solution.py:451
  135.2 7.2 %collective-permute-start.15 = (bf16[1,32,1152]{2,1,0:T(8,128)(2,1)S(1)}, bf16[1,32,1152]{2,1,0:T(8,128)(2,1)S(1)}, u32[]{:S(2)}, u32[]{:S(2)}) collective-permute-start(bf16[1,32,1152]{2,1,0:T(8,128)(2,1)S(1)} %get-tuple-element.108), channel_id=1, source_target_pairs={{0,2},{1,3},{2,4},{3,5},{4,6},{5,7},{6,0},{7,1},{8,10},{9,11},{10,... | collective-permute-start | bytes 221192 | tf_op jit(solution)/shard_map/ppermute | solution.py:451
  136.2 10.1 %collective-permute-start.16 = (bf16[1,32,1152]{2,1,0:T(8,128)(2,1)S(1)}, bf16[1,32,1152]{2,1,0:T(8,128)(2,1)S(1)}, u32[]{:S(2)}, u32[]{:S(2)}) collective-permute-start(bf16[1,32,1152]{2,1,0:T(8,128)(2,1)S(1)} %get-tuple-element.109), channel_id=1, source_target_pairs={{0,3},{1,2},{2,5},{3,4},{4,7},{5,6},{6,1},{7,0},{8,11},{9,10},{10,... | collective-permute-start | bytes 221192 | tf_op jit(solution)/shard_map/ppermute | solution.py:451
  136.5 9.8 %collective-permute-start.17 = (bf16[1,32,1152]{2,1,0:T(8,128)(2,1)S(1)}, bf16[1,32,1152]{2,1,0:T(8,128)(2,1)S(1)}, u32[]{:S(2)}, u32[]{:S(2)}) collective-permute-start(bf16[1,32,1152]{2,1,0:T(8,128)(2,1)S(1)} %get-tuple-element.110), channel_id=1, source_target_pairs={{0,4},{1,5},{2,6},{3,7},{4,0},{5,1},{6,2},{7,3},{8,12},{9,13},{10,... | collective-permute-start | bytes 221192 | tf_op jit(solution)/shard_map/ppermute | solution.py:451
  139.5 6.9 %collective-permute-start.18 = (bf16[1,32,1152]{2,1,0:T(8,128)(2,1)S(1)}, bf16[1,32,1152]{2,1,0:T(8,128)(2,1)S(1)}, u32[]{:S(2)}, u32[]{:S(2)}) collective-permute-start(bf16[1,32,1152]{2,1,0:T(8,128)(2,1)S(1)} %get-tuple-element.111), channel_id=1, source_target_pairs={{0,5},{1,4},{2,7},{3,6},{4,1},{5,0},{6,3},{7,2},{8,13},{9,12},{10,... | collective-permute-start | bytes 221192 | tf_op jit(solution)/shard_map/ppermute | solution.py:451
  140.1 6.3 %collective-permute-start.19 = (bf16[1,32,1152]{2,1,0:T(8,128)(2,1)S(1)}, bf16[1,32,1152]{2,1,0:T(8,128)(2,1)S(1)}, u32[]{:S(2)}, u32[]{:S(2)}) collective-permute-start(bf16[1,32,1152]{2,1,0:T(8,128)(2,1)S(1)} %get-tuple-element.112), channel_id=1, source_target_pairs={{0,6},{1,7},{2,0},{3,1},{4,2},{5,3},{6,4},{7,5},{8,14},{9,15},{10,... | collective-permute-start | bytes 221192 | tf_op jit(solution)/shard_map/ppermute | solution.py:451
  (27 other events, 339.9 us)

commit v3 on v2

--- a/solution.py
+++ b/solution.py
@@ -40,10 +40,12 @@
 
 
 def copy_all(pairs, sems):
-    copies = [pltpu.make_async_copy(src, dst, sems.at[n]) for n, (src, dst) in enumerate(pairs)]
+    return [pltpu.make_async_copy(src, dst, sems.at[n]) for n, (src, dst) in enumerate(pairs)]
+
+
+def start_all(copies):
     for copy in copies:
         copy.start()
-    return copies
 
 
 def wait_all(copies):
@@ -97,8 +99,22 @@
             pltpu.SemaphoreType.DMA((4,)),
         ],
         compiler_params=pltpu.CompilerParams(vmem_limit_bytes=40 * MIB),
+        cost_estimate=cost(0, 0),
         name="prepare",
     )(far(weight_qkv), far(weight_out))
+
+
+def regroup(x, outer, inner):
+    rows = x.shape[0]
+    to = lax.broadcasted_iota(jnp.int32, (rows, rows), 0)
+    at = lax.broadcasted_iota(jnp.int32, (rows, rows), 1)
+    wanted = to // 2 % outer * (2 * inner) + to // (2 * outer) * 2 + to % 2
+    return dot_nn((at == wanted).astype(BF16), x).astype(BF16)
+
+
+def group_rows():
+    per = HEADS // GROUPS
+    return [pl.ds((j * HEADS + g * per) * HP, HP * per) for g in range(GROUPS) for j in range(3)]
 
 
 def assemble(dst, f, own, part_of, pieces, from_ref, sems):
@@ -124,12 +140,12 @@
     copies = []
     for f in range(2):
         copies += assemble(x_ref, f, clips.at[f], f, pieces, from_ref, sems)
-    first = HP * HEADS // GROUPS
-    parts = [pl.ds(j * HEADS * HP, first) for j in range(3)]
-    parts += [pl.ds(j * HEADS * HP + first, HEADS * HP - first) for j in range(3)]
+    parts = group_rows()
     weights = copy_all([(wt_hbm.at[part], wt.at[part]) for part in parts], wsem)
     out_weight = copy_all([(wo_hbm, wo)], osem)
+    start_all(weights[:3])
     wait_all(copies)
+    start_all(weights[3:6])
     toks = x_ref.shape[0]
     frames = toks // 256
     per = HEADS // GROUPS
@@ -170,13 +186,17 @@
         att[pl.ds(HP * h, HP), cols] = (dot_nn(v, probs[h, :, cols]) * inverse[h, :, cols]).astype(BF16)
 
     wait_all(weights[:3])
+    start_all(weights[6:9])
     project(0)
-    wait_all(weights[3:])
     scores(0)
     for i in range(len(units)):
         h, f = units[i]
         if f == 0 and h % per == per - 2 and h // per + 1 < GROUPS:
-            project(h // per + 1)
+            g = h // per + 1
+            wait_all(weights[3 * g:3 * g + 3])
+            if g == 1:
+                start_all(weights[9:] + out_weight)
+            project(g)
         if f == 0 and h == HEADS // 2 + 1:
             half = pl.ds(0, HEADS // 2)
             saves = [pltpu.make_async_copy(probs.at[half], p_hbm.at[half], ssem.at[0])]
@@ -207,6 +227,8 @@
         def _():
             total[part] = jnp.zeros((256, total.shape[1]), BF16)
 
+        if f:
+            total[part] = regroup(total[part], sems.shape[1], 256 // (2 * sems.shape[1]))
         saves.append(pltpu.make_async_copy(total.at[part], out_ref, ssem.at[4 + f]))
         saves[-1].start()
     wait_all(saves)
@@ -239,7 +261,7 @@
             pltpu.VMEM(wt.shape, BF16),
             pltpu.VMEM(wo.shape, BF16),
             pltpu.VMEM((2 * toks, width), BF16),
-            pltpu.SemaphoreType.DMA((6,)),
+            pltpu.SemaphoreType.DMA((3 * GROUPS,)),
             pltpu.SemaphoreType.DMA((1,)),
             pltpu.SemaphoreType.DMA((6,)),
         ],
@@ -250,22 +272,35 @@
 
 
 def backward_kernel(scale, from_ref, keep_ref, inverse, wt_hbm, wo_hbm, x_hbm, qkv_hbm, p_hbm, cot_a, cot_b, *rest):
-    pieces, (ga_ref, gb_ref, c_ref, gatt, gqkv, gabuf, gpbuf, gsbuf, sems) = rest[:-16], rest[-16:-7]
-    x_ref, qkv, probs, wt, wo, total, lsem = rest[-7:]
+    pieces, (ga_ref, gb_ref, c_ref, gatt, gqkv, gabuf, gpbuf, gsbuf, sems) = rest[:-19], rest[-19:-10]
+    x_ref, qkv, probs, wt, wo, total, lsem, gsem, tsem, ssem = rest[-10:]
     copies = assemble(c_ref, 0, cot_a, 2, pieces, from_ref, sems) + assemble(c_ref, 1, cot_b, 0, [], from_ref, sems)
-    low, high = pl.ds(0, HEADS // 2), pl.ds(HEADS // 2, HEADS // 2)
-    pairs = [(wo_hbm, wo), (qkv_hbm, qkv), (p_hbm.at[low], probs.at[low]), (p_hbm.at[high], probs.at[high])]
-    loads = copy_all(pairs + [(x_hbm, x_ref), (wt_hbm, wt)], lsem)
+    per = HEADS // GROUPS
+    parts = group_rows()
+    heads = [pl.ds(g * per, per) for g in range(GROUPS)]
+    quarter = wt.shape[0] // GROUPS
+    rows = [pl.ds(g * quarter, quarter) for g in range(GROUPS)]
+    load_wo = copy_all([(wo_hbm, wo)], lsem)
+    loads = [
+        copy_all([(qkv_hbm.at[part], qkv.at[part]) for part in parts[3 * g:3 * g + 3]]
+                 + [(p_hbm.at[heads[g]], probs.at[heads[g]])], gsem.at[g])
+        for g in range(GROUPS)
+    ]
+    late = copy_all([(wt_hbm.at[part], wt.at[part]) for part in rows] + [(x_hbm, x_ref)], tsem)
+    start_all(load_wo)
     wait_all(copies)
+    start_all(loads[0])
     for f in range(2):
         part = c_ref[pl.ds(f * 256, 256)]
         c_ref[pl.ds(f * 256, 256)] = jnp.where(keep_ref[f] > 0, part, jnp.zeros_like(part))
     toks = x_ref.shape[0]
     frames = toks // 256
     third = HEADS * HP
-    wait_all(loads[:1])
+    wait_all(load_wo)
+    start_all(loads[1])
     gatt[...] = dot_nt(wo[...], c_ref[...])
-    wait_all(loads[1:3])
+    wait_all(loads[0])
+    start_all(late[:1])
     units = [(h, f) for h in range(HEADS) for f in range(frames)]
 
     def rows_of(h):
@@ -302,16 +337,20 @@
 
     reach(0)
     for i in range(len(units)):
-        if units[i] == (HEADS // 2, 0):
-            wait_all(loads[3:4])
         values(i)
         if i + 1 < len(units):
+            h, f = units[i + 1]
+            if f == 0 and h % per == 0:
+                g = h // per
+                wait_all(loads[g])
+                start_all(late[g:g + 1])
+                start_all(loads[g + 1] if g + 1 < GROUPS else late[GROUPS:])
             reach(i + 1)
         soften(i)
         if i:
             spread(i - 1)
     spread(len(units) - 1)
-    wait_all(loads[4:])
+    wait_all(late)
     gn = dot_tn(gqkv[...], wt[...])
     x = x_ref[...].astype(F32)
     mean = jnp.mean(x, axis=-1, keepdims=True)
@@ -321,7 +360,9 @@
     n = centered * inv
     gx = inv * (gn - jnp.mean(gn, axis=-1, keepdims=True) - n * jnp.mean(gn * n, axis=-1, keepdims=True))
     total[...] = (c_ref[...].astype(F32) + gx).astype(BF16)
-    wait_all(copy_all([(total.at[pl.ds(0, 256)], ga_ref), (total.at[pl.ds(256, 256)], gb_ref)], lsem))
+    saves = copy_all([(total.at[pl.ds(0, 256)], ga_ref), (total.at[pl.ds(256, 256)], gb_ref)], ssem)
+    start_all(saves)
+    wait_all(saves)
 
 
 def backward(cot_a, cot_b, pieces, origins, keep, wt, wo, kept, scale):
@@ -348,7 +389,10 @@
             pltpu.VMEM(wt.shape, BF16),
             pltpu.VMEM(wo.shape, BF16),
             pltpu.VMEM(x.shape, BF16),
-            pltpu.SemaphoreType.DMA((6,)),
+            pltpu.SemaphoreType.DMA((1,)),
+            pltpu.SemaphoreType.DMA((GROUPS, 4)),
+            pltpu.SemaphoreType.DMA((GROUPS + 1,)),
+            pltpu.SemaphoreType.DMA((2,)),
         ],
         compiler_params=pltpu.CompilerParams(vmem_limit_bytes=48 * MIB),
         cost_estimate=cost(4 * toks * (wt.size + wo.size) + 16 * wo.shape[0] * toks * toks, 2 * (wt.size + wo.size)),
@@ -376,10 +420,13 @@
     return lax.all_to_all(x.reshape(groups, -1, x.shape[-1]), "grp", 0, 0, tiled=True)
 
 
-def pack_kernel(leads, to_ref, *refs):
+def pack_kernel(leads, whole, to_ref, *refs):
     count = len(leads)
     sources, outs, sems = refs[:count], refs[count:-1], refs[-1]
     copies = []
+    if whole is not None:
+        copies.append(pltpu.make_async_copy(sources[-1].at[whole], outs[-1], sems.at[len(outs) - 1, 0]))
+        outs = outs[:-1]
     for n, out in enumerate(outs):
         at = to_ref[n + 1]
         for a, lead in enumerate(leads):
@@ -391,15 +438,18 @@
         copy.wait()
 
 
-def pack(sources, leads, targets):
+def pack(sources, leads, targets, whole=None):
     n = targets.shape[0]
     block = sources[0].shape[-2:]
+    shapes = (jax.ShapeDtypeStruct((len(leads),) + block, BF16),) * (n - 1)
+    if whole is not None:
+        shapes += (jax.ShapeDtypeStruct(sources[-1].shape[1:], BF16),)
     return pl.pallas_call(
-        functools.partial(pack_kernel, leads),
-        out_shape=(jax.ShapeDtypeStruct((len(leads),) + block, BF16),) * (n - 1),
+        functools.partial(pack_kernel, leads, whole),
+        out_shape=shapes,
         in_specs=[IN_SMEM] + [ANYWHERE] * len(sources),
-        out_specs=(IN_VMEM,) * (n - 1),
-        scratch_shapes=[pltpu.SemaphoreType.DMA((n - 1, len(leads)))],
+        out_specs=(IN_VMEM,) * len(shapes),
+        scratch_shapes=[pltpu.SemaphoreType.DMA((len(shapes), len(leads)))],
         compiler_params=pltpu.CompilerParams(vmem_limit_bytes=12 * MIB),
         name="pack",
     )(targets, *[far(x) for x in sources])
@@ -407,34 +457,40 @@
 
 def unpack_kernel(picks, from_ref, *refs):
     owns = len(picks)
-    sources, (out, held, in_sems, out_sems) = refs[:-4], refs[-4:]
+    sources, (*outs, held, in_sems, out_sems) = refs[:-5], refs[-5:]
     own, pieces = sources[:owns], sources[owns:]
+    frames = in_sems.shape[1]
     reads, writes = [], []
     for a, pick in enumerate(picks):
-        for n in range(in_sems.shape[1]):
-            at = from_ref[n]
-            first, clip = pick
-            src = pieces[first + n - 1].at[clip] if n else own[a].at[at]
+        for n in range(frames):
+            if pick is None:
+                at, src = n, own[a].at[n]
+            else:
+                at = from_ref[n]
+                src = pieces[n - 1].at[pick] if n else own[a].at[at]
             reads.append(pltpu.make_async_copy(src, held.at[a, n], in_sems.at[a, n]))
-            writes.append(pltpu.make_async_copy(held.at[a, n], out.at[a, at], out_sems.at[a, n]))
-    for read in reads:
-        read.start()
-    for read, write in zip(reads, writes):
-        read.wait()
-        write.start()
+            writes.append(pltpu.make_async_copy(held.at[a, n], outs[a // 2].at[a % 2, at], out_sems.at[a, n]))
+    start_all(reads)
+    for a, pick in enumerate(picks):
+        mine = slice(a * frames, (a + 1) * frames)
+        wait_all(reads[mine])
+        if pick is None:
+            rows = held[a].reshape(-1, held.shape[-1])
+            held[a] = regroup(rows, rows.shape[0] // (2 * frames), frames).reshape(held.shape[1:])
+        start_all(writes[mine])
     wait_all(writes)
 
 
 def unpack(own, pieces, picks, origins):
     n = origins.shape[0]
-    shape = (len(picks),) + own[0].shape
+    shape = own[0].shape
     return pl.pallas_call(
         functools.partial(unpack_kernel, picks),
-        out_shape=pltpu.HBM(shape, BF16),
+        out_shape=(pltpu.HBM((2,) + shape, BF16),) * 2,
         in_specs=[IN_SMEM] + [ANYWHERE] * (len(own) + len(pieces)),
-        out_specs=ANYWHERE,
+        out_specs=(ANYWHERE,) * 2,
         scratch_shapes=[
-            pltpu.VMEM(shape, BF16),
+            pltpu.VMEM((len(picks),) + shape, BF16),
             pltpu.SemaphoreType.DMA((len(picks), n)),
             pltpu.SemaphoreType.DMA((len(picks), n)),
         ],
@@ -450,16 +506,6 @@
         pairs = [(i, (i // 2 + n // 2) % chips * 2 + (i % 2 ^ n % 2)) for i in range(size)]
         out.append(lax.ppermute(x, "sp", pairs))
     return out
-
-
-def settle(pieces, *others):
-    across = [n for n in range(len(pieces)) if (n + 1) // 2 == (len(pieces) + 1) // 4]
-    near = [n for n in range(len(pieces)) if n not in across]
-    *held, rest = lax.optimization_barrier((*[pieces[n] for n in near], others))
-    pieces = list(pieces)
-    for n, piece in zip(near, held):
-        pieces[n] = piece
-    return (pieces, *rest)
 
 
 def on_device(clips, counts, dest, weight_qkv, weight_out, cotangent):
@@ -478,11 +524,14 @@
     keep_a, keep_b = keep[0:1], keep[1:2]
 
     block = clips.shape[1:]
-    cot_b = spread(cotangent[1], groups)
-    pieces = exchange(pack((clips, clips, cotangent), ((0,), (1,), (0,)), targets), size)
+    width = block[-1]
+    *sends, cot_b = pack((clips, clips, cotangent), ((0,), (1,), (0,)), targets, whole=1)
+    cot_b = spread(cot_b, groups)
+    pieces = exchange(sends, size)
+    cot_b = shuffle(cot_b, dest)
+    weight_qkv, cot_b = lax.optimization_barrier((weight_qkv, cot_b))
     wt, wo = prepare(weight_qkv, weight_out)
-    pieces, cot_b, wt = settle(pieces, cot_b, wt)
-    cot_b = spread(shuffle(cot_b, dest), groups).reshape(block)
+    cot_b = spread(cot_b, groups).reshape(block)
     cot_b, wt = lax.optimization_barrier((cot_b, wt))
     out_a, out_b, *kept = forward(clips, pieces, origins, keep, wt, wo, scale)
     cot_b = lax.all_to_all(cot_b, "sp", 0, 0, tiled=True)
@@ -490,14 +539,11 @@
     out_b = spread(out_b, groups)
     grad_a, grad_b = backward(cotangent[0], cot_b, pieces, origins, keep, wt, wo, kept, scale)
     grad_a, grad_b, out_a = grad_a.reshape(block), grad_b.reshape(block), out_a.reshape(block)
-    sends = pack((grad_a, grad_b, out_a), (None, None, None), targets)
-    out_b, sends = lax.optimization_barrier((out_b, sends))
-    back = exchange(sends, size)
-    out_b = spread(shuffle(out_b, source), groups).reshape(block)
-    back, out_b = settle(back, out_b)
-    late = exchange(pack((out_b,), (None,), targets), size)
-    grads = unpack((grad_a, grad_b), back, ((0, 0), (0, 1)), origins)
-    outputs = unpack((out_a, out_b), back + late, ((0, 2), (len(back), 0)), origins)
+    out_b, grad_a = lax.optimization_barrier((out_b, grad_a))
+    out_b = shuffle(out_b, source).reshape(groups * size, -1, width)
+    out_b = lax.all_to_all(out_b, ("grp", "sp"), 0, 0, tiled=True).reshape(block)
+    back = exchange(pack((grad_a, grad_b, out_a), (None, None, None), targets), size)
+    grads, outputs = unpack((grad_a, grad_b, out_a, out_b), back, (0, 1, 2, None), origins)
     return (outputs, grads)
 
 

time: 153 us -> 140 us (0.915)
  starting transfers between devices: 68.5 us -> 55.3 us
  Pallas kernels: 59.5 us -> 55.2 us
  waiting for transfers between devices: 17.7 us -> 21.9 us
    ppermute x21 -> x14, starting transfers between devices: 38.4 us -> 23.1 us  [exchange(): out.append(lax.ppermute(x, 'sp', pairs))]
    all_to_all x0 -> x1, starting transfers between devices: none -> 9.72 us  [on_device(): lax.all_to_all(out_b, ('grp', 'sp'), 0, 0, tiled=True).reshape(block)]
    ppermute x21 -> x14, waiting for transfers between devices: 9.83 us -> 18.7 us  [exchange(): out.append(lax.ppermute(x, 'sp', pairs))]
    all_to_all x4 -> x3, starting transfers between devices: 24.7 us -> 18.7 us  [spread(): lax.all_to_all(x.reshape(groups, -1, x.shape[-1]), 'grp', 0, 0, tiled=True)]
    all_to_all x4 -> x3, waiting for transfers between devices: 7.83 us -> 3.22 us  [spread(): lax.all_to_all(x.reshape(groups, -1, x.shape[-1]), 'grp', 0, 0, tiled=True)]
    pallas_call x5 -> x3, Pallas kernels: 11.7 us -> 9.21 us  [the longest x2 5.26 us: pack(): pl.pallas_call(functools.partial(pack_kernel, leads, whole), out_shape=sh...]
    reshape x0 -> x2, local copies, waits for them, and re-layouts: none -> 2.07 us  [the longest x1 1.04 us: on_device(): lax.all_to_all(out_b, ('grp', 'sp'), 0, 0, tiled=True).reshape(block)]
    all_to_all x1, starting transfers between devices: 5.36 us -> 3.82 us  [on_device(): cot_b = lax.all_to_all(cot_b, 'sp', 0, 0, tiled=True)]
  transfers between devices with their start and end apart: 26 -> 19, of which waited for: 8 -> 5; matrix products, arithmetic and copies ran while one was open for 0% -> 2% of each run, Pallas kernels for 36% -> 34%
where the time goes in v3:
time: 140 us; the launch traced here: 139 us
  starting transfers between devices  55.3 us (40%)
  Pallas kernels  55.2 us (39%)
  waiting for transfers between devices  21.9 us (16%)
  local copies, waits for them, and re-layouts  5.15 us (4%)
    ppermute x14, starting transfers between devices, exchange(): out.append(lax.ppermute(x, 'sp', pairs))  23.1 us
    pallas_call x1, Pallas kernels, backward(): pl.pallas_call(functools.partial(backward_kernel, scale), out_shape=(out,...  20.7 us
    all_to_all x3, starting transfers between devices, spread(): lax.all_to_all(x.reshape(groups, -1, x.shape[-1]), 'grp', 0, 0, tiled=True)  18.7 us
    ppermute x14, waiting for transfers between devices, exchange(): out.append(lax.ppermute(x, 'sp', pairs))  18.7 us
    pallas_call x1, Pallas kernels, forward(): pl.pallas_call(functools.partial(forward_kernel, scale), out_shape=(out,...  15.9 us
    all_to_all x1, starting transfers between devices, on_device(): lax.all_to_all(out_b, ('grp', 'sp'), 0, 0, tiled=True).reshape(block)  9.72 us
    pallas_call x1, Pallas kernels, prepare(): pl.pallas_call(prepare_kernel, out_shape=(pltpu.HBM((3 * HEADS * HP, widt...  7.37 us
    pallas_call x2, Pallas kernels, pack(): pl.pallas_call(functools.partial(pack_kernel, leads, whole), out_shape=sh...  5.26 us
  transfers between devices with their start and end apart: 19, of which 5 were waited for; matrix products, arithmetic and copies ran while one was open for 2% of the time, Pallas kernels for 34%

profile of v3, /device:TPU:1, one launch (start us, length us, event | category | flops | bytes accessed | tf_op | source)
XLA Modules:
  0.0 138.9 jit_solution(1697687904739318482)
XLA Ops:
  0.7 3.1 %pack.2 = (bf16[3,32,1152]{2,1,0:T(8,128)(2,1)S(1)}, bf16[3,32,1152]{2,1,0:T(8,128)(2,1)S(1)}, bf16[3,32,1152]{2,1,0:T(8,128)(2,1)S(1)}, bf16[3,32,1152]{2,1,0:T...) custom-call(s32[8]{0:T(128)S(1)} %fusion.3.to_ref, ...), custom_call_target="tpu_custom_call" | custom-call | tf_op jit(solution)/shard_map/pack/pallas_call | solution.py:447
  3.8 7.7 %all-to-all-start = ((bf16[16,16,1152]{2,1,0:T(8,128)(2,1)}), bf16[16,16,1152]{2,1,0:T(8,128)(2,1)S(1)}, u32[]{:S(2)}, u32[]{:S(2)}) async-start(bf16[16,16,1152]{2,1,0:T(8,128)(2,1)} %bitcast), calls=%async_computation | async-start | bytes 1179648 | tf_op jit(solution)/shard_map/all_to_all | solution.py:420
  12.6 1.7 %collective-permute-start.1 = (bf16[3,32,1152]{2,1,0:T(8,128)(2,1)S(1)}, bf16[3,32,1152]{2,1,0:T(8,128)(2,1)}, u32[]{:S(2)}, u32[]{:S(2)}) collective-permute-start(bf16[3,32,1152]{2,1,0:T(8,128)(2,1)S(1)} %get-tuple-element.45), channel_id=1, source_target_pairs={{0,2},{1,3},{2,4},{3,5},{4,6},{5,7},{6,0},{7,1},{8,10},{9,11},{10,... | collective-permute-start | bytes 663560 | tf_op jit(solution)/shard_map/ppermute | solution.py:507
  14.2 1.9 %collective-permute-start.2 = (bf16[3,32,1152]{2,1,0:T(8,128)(2,1)S(1)}, bf16[3,32,1152]{2,1,0:T(8,128)(2,1)}, u32[]{:S(2)}, u32[]{:S(2)}) collective-permute-start(bf16[3,32,1152]{2,1,0:T(8,128)(2,1)S(1)} %get-tuple-element.46), channel_id=1, source_target_pairs={{0,3},{1,2},{2,5},{3,4},{4,7},{5,6},{6,1},{7,0},{8,11},{9,10},{10,... | collective-permute-start | bytes 663560 | tf_op jit(solution)/shard_map/ppermute | solution.py:507
  17.6 1.8 %collective-permute-start.4 = (bf16[3,32,1152]{2,1,0:T(8,128)(2,1)S(1)}, bf16[3,32,1152]{2,1,0:T(8,128)(2,1)}, u32[]{:S(2)}, u32[]{:S(2)}) collective-permute-start(bf16[3,32,1152]{2,1,0:T(8,128)(2,1)S(1)} %get-tuple-element.48), channel_id=1, source_target_pairs={{0,5},{1,4},{2,7},{3,6},{4,1},{5,0},{6,3},{7,2},{8,13},{9,12},{10,... | collective-permute-start | bytes 663560 | tf_op jit(solution)/shard_map/ppermute | solution.py:507
  19.4 3.2 %all-to-all-done.x_ref = bf16[16,16,1152]{2,1,0:T(8,128)(2,1)S(1)} async-done(((bf16[16,16,1152]{2,1,0:T(8,128)(2,1)}), bf16[16,16,1152]{2,1,0:T(8,128)(2,1)S(1)}, u32[]{:S(2)}, u32[]{:S(2)}) %all-to-all-start) | async-done | bytes 589856 | tf_op jit(solution)/shard_map/all_to_all | solution.py:420
  24.0 4.3 %all-to-all-start.1 = ((bf16[16,16,1152]{2,1,0:T(8,128)(2,1)}), bf16[16,16,1152]{2,1,0:T(8,128)(2,1)}, u32[]{:S(2)}, u32[]{:S(2)}) async-start(bf16[16,16,1152]{2,1,0:T(8,128)(2,1)} %shuffle.2), calls=%async_computation.1 | async-start | bytes 1179648 | tf_op jit(solution)/shard_map/all_to_all | solution.py:420
  29.2 3.8 %collective-permute-start.5 = (bf16[3,32,1152]{2,1,0:T(8,128)(2,1)S(1)}, bf16[3,32,1152]{2,1,0:T(8,128)(2,1)S(1)}, u32[]{:S(2)}, u32[]{:S(2)}) collective-permute-start(bf16[3,32,1152]{2,1,0:T(8,128)(2,1)S(1)} %get-tuple-element.49), channel_id=1, source_target_pairs={{0,6},{1,7},{2,0},{3,1},{4,2},{5,3},{6,4},{7,5},{8,14},{9,15},{10,... | collective-permute-start | bytes 663560 | tf_op jit(solution)/shard_map/ppermute | solution.py:507
  33.0 2.4 %collective-permute-start.6 = (bf16[3,32,1152]{2,1,0:T(8,128)(2,1)S(1)}, bf16[3,32,1152]{2,1,0:T(8,128)(2,1)S(1)}, u32[]{:S(2)}, u32[]{:S(2)}) collective-permute-start(bf16[3,32,1152]{2,1,0:T(8,128)(2,1)S(1)} %get-tuple-element.50), channel_id=1, source_target_pairs={{0,7},{1,6},{2,1},{3,0},{4,3},{5,2},{6,5},{7,4},{8,15},{9,14},{10,... | collective-permute-start | bytes 663560 | tf_op jit(solution)/shard_map/ppermute | solution.py:507
  35.6 7.4 %prepare.1 = (bf16[3840,1152]{1,0:T(8,128)(2,1)}, bf16[1280,1152]{1,0:T(8,128)(2,1)}) custom-call(bf16[1152,3456]{1,0:T(8,128)(2,1)} %wq_hbm, bf16[1152,1152]{1,0:T(8,128)(2,1)} %wo_hbm.1), custom_call_target="tpu_custom_call" | custom-call | tf_op jit(solution)/shard_map/prepare/pallas_call | solution.py:88
  43.0 3.8 %all-to-all-start.2 = ((bf16[8,32,1152]{2,1,0:T(8,128)(2,1)}), bf16[8,32,1152]{2,1,0:T(8,128)(2,1)S(1)}, u32[]{:S(2)}, u32[]{:S(2)}) async-start(bf16[8,32,1152]{2,1,0:T(8,128)(2,1)} %bitcast.1), calls=%async_computation.2 | async-start | bytes 1179648 | tf_op jit(solution)/shard_map/all_to_all | solution.py:537
  47.6 15.9 %forward.1 = (bf16[256,1152]{1,0:T(8,128)(2,1)}, bf16[256,1152]{1,0:T(8,128)(2,1)}, bf16[512,1152]{1,0:T(8,128)(2,1)}, bf16[3840,512]{1,0:T(8,128)(2,1)}, bf16[1...) custom-call(s32[8]{0:T(128)S(1)} %fusion.1.from_ref, s32[2]{0:T(128)S(1)} %compare_convert_fusion.keep_ref, ...), custom_call_target="tpu_custom_call" | custom-call | flops 6710886400 | bytes 11796480 | tf_op jit(solution)/shard_map/forward/pallas_call | solution.py:241
  63.6 6.7 %all-to-all-start.3 = ((bf16[16,16,1152]{2,1,0:T(8,128)(2,1)}), bf16[16,16,1152]{2,1,0:T(8,128)(2,1)S(1)}, u32[]{:S(2)}, u32[]{:S(2)}) async-start(bf16[16,16,1152]{2,1,0:T(8,128)(2,1)} %bitcast.14), calls=%async_computation.3 | async-start | bytes 1179648 | tf_op jit(solution)/shard_map/all_to_all | solution.py:420
  70.3 20.7 %backward.1 = (bf16[256,1152]{1,0:T(8,128)(2,1)}, bf16[256,1152]{1,0:T(8,128)(2,1)}) custom-call(s32[8]{0:T(128)S(1)} %fusion.1.from_ref, s32[2]{0:T(128)S(1)} %compare_convert_fusion.keep_ref, f32[16,1,512]{2,1,0:T(1,128)S(1)} %get-tuple-element.53.inverse, bf16[3840,1152]{1,0:T(8,128)(2,1)} %get-tuple-element.42.wt_hbm, ...), custom_call_target="tpu_custom_call" | custom-call | flops 7381975040 | bytes 11796480 | tf_op jit(solution)/shard_map/backward/pallas_call | solution.py:373
  92.7 9.7 %all-to-all-start.4 = ((bf16[128,2,1152]{2,1,0:T(2,128)(2,1)}), bf16[128,2,1152]{2,1,0:T(2,128)(2,1)S(1)}, u32[]{:S(2)}, u32[]{:S(2)}) async-start(bf16[128,2,1152]{2,1,0:T(2,128)(2,1)} %reshape.35), calls=%async_computation.4 | async-start | bytes 1179648 | tf_op jit(solution)/shard_map/all_to_all | solution.py:544
  102.4 2.2 %pack.3 = (bf16[3,32,1152]{2,1,0:T(8,128)(2,1)S(1)}, bf16[3,32,1152]{2,1,0:T(8,128)(2,1)S(1)}, bf16[3,32,1152]{2,1,0:T(8,128)(2,1)S(1)}, bf16[3,32,1152]{2,1,0:T...) custom-call(s32[8]{0:T(128)S(1)} %fusion.3.to_ref, ...), custom_call_target="tpu_custom_call" | custom-call | tf_op jit(solution)/shard_map/pack/pallas_call | solution.py:447
  106.6 1.8 %collective-permute-start.9 = (bf16[3,32,1152]{2,1,0:T(8,128)(2,1)S(1)}, bf16[3,32,1152]{2,1,0:T(8,128)(2,1)S(1)}, u32[]{:S(2)}, u32[]{:S(2)}) collective-permute-start(bf16[3,32,1152]{2,1,0:T(8,128)(2,1)S(1)} %get-tuple-element.65), channel_id=1, source_target_pairs={{0,3},{1,2},{2,5},{3,4},{4,7},{5,6},{6,1},{7,0},{8,11},{9,10},{10,... | collective-permute-start | bytes 663560 | tf_op jit(solution)/shard_map/ppermute | solution.py:507
  108.4 1.5 %collective-permute-start.10 = (bf16[3,32,1152]{2,1,0:T(8,128)(2,1)S(1)}, bf16[3,32,1152]{2,1,0:T(8,128)(2,1)S(1)}, u32[]{:S(2)}, u32[]{:S(2)}) collective-permute-start(bf16[3,32,1152]{2,1,0:T(8,128)(2,1)S(1)} %get-tuple-element.66), channel_id=1, source_target_pairs={{0,4},{1,5},{2,6},{3,7},{4,0},{5,1},{6,2},{7,3},{8,12},{9,13},{10,... | collective-permute-start | bytes 663560 | tf_op jit(solution)/shard_map/ppermute | solution.py:507
  109.9 1.7 %collective-permute-start.11 = (bf16[3,32,1152]{2,1,0:T(8,128)(2,1)S(1)}, bf16[3,32,1152]{2,1,0:T(8,128)(2,1)S(1)}, u32[]{:S(2)}, u32[]{:S(2)}) collective-permute-start(bf16[3,32,1152]{2,1,0:T(8,128)(2,1)S(1)} %get-tuple-element.67), channel_id=1, source_target_pairs={{0,5},{1,4},{2,7},{3,6},{4,1},{5,0},{6,3},{7,2},{8,13},{9,12},{10,... | collective-permute-start | bytes 663560 | tf_op jit(solution)/shard_map/ppermute | solution.py:507
  112.8 6.3 %collective-permute-done.8.refs_5_ = bf16[3,32,1152]{2,1,0:T(8,128)(2,1)S(1)} collective-permute-done((bf16[3,32,1152]{2,1,0:T(8,128)(2,1)S(1)}, bf16[3,32,1152]{2,1,0:T(8,128)(2,1)S(1)}, u32[]{:S(2)}, u32[]{:S(2)}) %collective-permute-start.8) | collective-permute-done | bytes 221216 | tf_op jit(solution)/shard_map/ppermute | solution.py:507
  121.0 2.8 %collective-permute-done.9.refs_6_ = bf16[3,32,1152]{2,1,0:T(8,128)(2,1)S(1)} collective-permute-done((bf16[3,32,1152]{2,1,0:T(8,128)(2,1)S(1)}, bf16[3,32,1152]{2,1,0:T(8,128)(2,1)S(1)}, u32[]{:S(2)}, u32[]{:S(2)}) %collective-permute-start.9) | collective-permute-done | bytes 221216 | tf_op jit(solution)/shard_map/ppermute | solution.py:507
  123.8 4.7 %collective-permute-done.10.refs_7_ = bf16[3,32,1152]{2,1,0:T(8,128)(2,1)S(1)} collective-permute-done((bf16[3,32,1152]{2,1,0:T(8,128)(2,1)S(1)}, bf16[3,32,1152]{2,1,0:T(8,128)(2,1)S(1)}, u32[]{:S(2)}, u32[]{:S(2)}) %collective-permute-start.10) | collective-permute-done | bytes 221216 | tf_op jit(solution)/shard_map/ppermute | solution.py:507
  128.6 4.7 %collective-permute-done.11.refs_8_ = bf16[3,32,1152]{2,1,0:T(8,128)(2,1)S(1)} collective-permute-done((bf16[3,32,1152]{2,1,0:T(8,128)(2,1)S(1)}, bf16[3,32,1152]{2,1,0:T(8,128)(2,1)S(1)}, u32[]{:S(2)}, u32[]{:S(2)}) %collective-permute-start.11) | collective-permute-done | bytes 221216 | tf_op jit(solution)/shard_map/ppermute | solution.py:507
  134.8 4.0 %unpack.1 = (bf16[2,8,32,1152]{3,2,1,0:T(8,128)(2,1)}, bf16[2,8,32,1152]{3,2,1,0:T(8,128)(2,1)}) custom-call(s32[8]{0:T(128)S(1)} %fusion.1.from_ref, bf16[8,32,1152]{2,1,0:T(8,128)(2,1)} %bitcast.11, bf16[8,32,1152]{2,1,0:T(8,128)(2,1)} %bitcast.13, bf16[8,32,1152]{2,1,0:T(8,128)(2,1)} %bitcast.9, bf16[8,32,1152]{2,1,0:T(8,128)(2,1)} %reshape.36.refs_3_, ...), custom_call_target="tpu_custom_call" | custom-call | tf_op jit(solution)/shard_map/unpack/pallas_call | solution.py:487
  (57 shorter events, 13.9 us)
Async XLA Ops:
  0.6 22.0 %copy-start = (s32[16]{0:T(128)S(1)}, s32[16]{0:T(128)}, u32[]{:S(2)}) copy-start(s32[16]{0:T(128)} %index_ref.1) | copy-start | bytes 196
  3.8 24.5 %copy-start.1 = (bf16[2,8,32,1152]{3,2,1,0:T(8,128)(2,1)S(1)}, bf16[2,8,32,1152]{3,2,1,0:T(8,128)(2,1)}, u32[]{:S(2)}) copy-start(bf16[2,8,32,1152]{3,2,1,0:T(8,128)(2,1)} %refs_2_.1) | copy-start | bytes 3538948
  3.8 31.6 %copy-start.10 = (s32[32]{0:T(128)S(1)}, s32[32]{0:T(128)}, u32[]{:S(2)}) copy-start(s32[32]{0:T(128)} %param.7) | copy-start | bytes 388
  3.8 18.8 %all-to-all-start = ((bf16[16,16,1152]{2,1,0:T(8,128)(2,1)}), bf16[16,16,1152]{2,1,0:T(8,128)(2,1)S(1)}, u32[]{:S(2)}, u32[]{:S(2)}) async-start(bf16[16,16,1152]{2,1,0:T(8,128)(2,1)} %bitcast), calls=%async_computation | async-start | bytes 1179648 | tf_op jit(solution)/shard_map/all_to_all | solution.py:420
  11.5 17.6 %collective-permute-start = (bf16[3,32,1152]{2,1,0:T(8,128)(2,1)S(1)}, bf16[3,32,1152]{2,1,0:T(8,128)(2,1)S(1)}, u32[]{:S(2)}, u32[]{:S(2)}) collective-permute-start(bf16[3,32,1152]{2,1,0:T(8,128)(2,1)S(1)} %get-tuple-element.44), channel_id=1, source_target_pairs={{0,1},{1,0},{2,3},{3,2},{4,5},{5,4},{6,7},{7,6},{8,9},{9,8},{10,11... | collective-permute-start | bytes 663560 | tf_op jit(solution)/shard_map/ppermute | solution.py:507
  12.6 20.4 %collective-permute-start.1 = (bf16[3,32,1152]{2,1,0:T(8,128)(2,1)S(1)}, bf16[3,32,1152]{2,1,0:T(8,128)(2,1)}, u32[]{:S(2)}, u32[]{:S(2)}) collective-permute-start(bf16[3,32,1152]{2,1,0:T(8,128)(2,1)S(1)} %get-tuple-element.45), channel_id=1, source_target_pairs={{0,2},{1,3},{2,4},{3,5},{4,6},{5,7},{6,0},{7,1},{8,10},{9,11},{10,... | collective-permute-start | bytes 663560 | tf_op jit(solution)/shard_map/ppermute | solution.py:507
  14.2 32.6 %collective-permute-start.2 = (bf16[3,32,1152]{2,1,0:T(8,128)(2,1)S(1)}, bf16[3,32,1152]{2,1,0:T(8,128)(2,1)}, u32[]{:S(2)}, u32[]{:S(2)}) collective-permute-start(bf16[3,32,1152]{2,1,0:T(8,128)(2,1)S(1)} %get-tuple-element.46), channel_id=1, source_target_pairs={{0,3},{1,2},{2,5},{3,4},{4,7},{5,6},{6,1},{7,0},{8,11},{9,10},{10,... | collective-permute-start | bytes 663560 | tf_op jit(solution)/shard_map/ppermute | solution.py:507
  16.1 30.7 %collective-permute-start.3 = (bf16[3,32,1152]{2,1,0:T(8,128)(2,1)S(1)}, bf16[3,32,1152]{2,1,0:T(8,128)(2,1)}, u32[]{:S(2)}, u32[]{:S(2)}) collective-permute-start(bf16[3,32,1152]{2,1,0:T(8,128)(2,1)S(1)} %get-tuple-element.47), channel_id=1, source_target_pairs={{0,4},{1,5},{2,6},{3,7},{4,0},{5,1},{6,2},{7,3},{8,12},{9,13},{10,... | collective-permute-start | bytes 663560 | tf_op jit(solution)/shard_map/ppermute | solution.py:507
  17.6 29.3 %collective-permute-start.4 = (bf16[3,32,1152]{2,1,0:T(8,128)(2,1)S(1)}, bf16[3,32,1152]{2,1,0:T(8,128)(2,1)}, u32[]{:S(2)}, u32[]{:S(2)}) collective-permute-start(bf16[3,32,1152]{2,1,0:T(8,128)(2,1)S(1)} %get-tuple-element.48), channel_id=1, source_target_pairs={{0,5},{1,4},{2,7},{3,6},{4,1},{5,0},{6,3},{7,2},{8,13},{9,12},{10,... | collective-permute-start | bytes 663560 | tf_op jit(solution)/shard_map/ppermute | solution.py:507
  24.0 19.0 %all-to-all-start.1 = ((bf16[16,16,1152]{2,1,0:T(8,128)(2,1)}), bf16[16,16,1152]{2,1,0:T(8,128)(2,1)}, u32[]{:S(2)}, u32[]{:S(2)}) async-start(bf16[16,16,1152]{2,1,0:T(8,128)(2,1)} %shuffle.2), calls=%async_computation.1 | async-start | bytes 1179648 | tf_op jit(solution)/shard_map/all_to_all | solution.py:420
  29.2 17.7 %collective-permute-start.5 = (bf16[3,32,1152]{2,1,0:T(8,128)(2,1)S(1)}, bf16[3,32,1152]{2,1,0:T(8,128)(2,1)S(1)}, u32[]{:S(2)}, u32[]{:S(2)}) collective-permute-start(bf16[3,32,1152]{2,1,0:T(8,128)(2,1)S(1)} %get-tuple-element.49), channel_id=1, source_target_pairs={{0,6},{1,7},{2,0},{3,1},{4,2},{5,3},{6,4},{7,5},{8,14},{9,15},{10,... | collective-permute-start | bytes 663560 | tf_op jit(solution)/shard_map/ppermute | solution.py:507
  33.0 13.9 %collective-permute-start.6 = (bf16[3,32,1152]{2,1,0:T(8,128)(2,1)S(1)}, bf16[3,32,1152]{2,1,0:T(8,128)(2,1)S(1)}, u32[]{:S(2)}, u32[]{:S(2)}) collective-permute-start(bf16[3,32,1152]{2,1,0:T(8,128)(2,1)S(1)} %get-tuple-element.50), channel_id=1, source_target_pairs={{0,7},{1,6},{2,1},{3,0},{4,3},{5,2},{6,5},{7,4},{8,15},{9,14},{10,... | collective-permute-start | bytes 663560 | tf_op jit(solution)/shard_map/ppermute | solution.py:507
  43.0 20.6 %all-to-all-start.2 = ((bf16[8,32,1152]{2,1,0:T(8,128)(2,1)}), bf16[8,32,1152]{2,1,0:T(8,128)(2,1)S(1)}, u32[]{:S(2)}, u32[]{:S(2)}) async-start(bf16[8,32,1152]{2,1,0:T(8,128)(2,1)} %bitcast.1), calls=%async_computation.2 | async-start | bytes 1179648 | tf_op jit(solution)/shard_map/all_to_all | solution.py:537
  63.6 27.5 %all-to-all-start.3 = ((bf16[16,16,1152]{2,1,0:T(8,128)(2,1)}), bf16[16,16,1152]{2,1,0:T(8,128)(2,1)S(1)}, u32[]{:S(2)}, u32[]{:S(2)}) async-start(bf16[16,16,1152]{2,1,0:T(8,128)(2,1)} %bitcast.14), calls=%async_computation.3 | async-start | bytes 1179648 | tf_op jit(solution)/shard_map/all_to_all | solution.py:420
  92.7 27.3 %all-to-all-start.4 = ((bf16[128,2,1152]{2,1,0:T(2,128)(2,1)}), bf16[128,2,1152]{2,1,0:T(2,128)(2,1)S(1)}, u32[]{:S(2)}, u32[]{:S(2)}) async-start(bf16[128,2,1152]{2,1,0:T(2,128)(2,1)} %reshape.35), calls=%async_computation.4 | async-start | bytes 1179648 | tf_op jit(solution)/shard_map/all_to_all | solution.py:544
  104.6 6.9 %collective-permute-start.7 = (bf16[3,32,1152]{2,1,0:T(8,128)(2,1)S(1)}, bf16[3,32,1152]{2,1,0:T(8,128)(2,1)S(1)}, u32[]{:S(2)}, u32[]{:S(2)}) collective-permute-start(bf16[3,32,1152]{2,1,0:T(8,128)(2,1)S(1)} %get-tuple-element.63), channel_id=1, source_target_pairs={{0,1},{1,0},{2,3},{3,2},{4,5},{5,4},{6,7},{7,6},{8,9},{9,8},{10,11... | collective-permute-start | bytes 663560 | tf_op jit(solution)/shard_map/ppermute | solution.py:507
  105.8 13.3 %collective-permute-start.8 = (bf16[3,32,1152]{2,1,0:T(8,128)(2,1)S(1)}, bf16[3,32,1152]{2,1,0:T(8,128)(2,1)S(1)}, u32[]{:S(2)}, u32[]{:S(2)}) collective-permute-start(bf16[3,32,1152]{2,1,0:T(8,128)(2,1)S(1)} %get-tuple-element.64), channel_id=1, source_target_pairs={{0,2},{1,3},{2,4},{3,5},{4,6},{5,7},{6,0},{7,1},{8,10},{9,11},{10,... | collective-permute-start | bytes 663560 | tf_op jit(solution)/shard_map/ppermute | solution.py:507
  106.6 17.3 %collective-permute-start.9 = (bf16[3,32,1152]{2,1,0:T(8,128)(2,1)S(1)}, bf16[3,32,1152]{2,1,0:T(8,128)(2,1)S(1)}, u32[]{:S(2)}, u32[]{:S(2)}) collective-permute-start(bf16[3,32,1152]{2,1,0:T(8,128)(2,1)S(1)} %get-tuple-element.65), channel_id=1, source_target_pairs={{0,3},{1,2},{2,5},{3,4},{4,7},{5,6},{6,1},{7,0},{8,11},{9,10},{10,... | collective-permute-start | bytes 663560 | tf_op jit(solution)/shard_map/ppermute | solution.py:507
  108.4 20.2 %collective-permute-start.10 = (bf16[3,32,1152]{2,1,0:T(8,128)(2,1)S(1)}, bf16[3,32,1152]{2,1,0:T(8,128)(2,1)S(1)}, u32[]{:S(2)}, u32[]{:S(2)}) collective-permute-start(bf16[3,32,1152]{2,1,0:T(8,128)(2,1)S(1)} %get-tuple-element.66), channel_id=1, source_target_pairs={{0,4},{1,5},{2,6},{3,7},{4,0},{5,1},{6,2},{7,3},{8,12},{9,13},{10,... | collective-permute-start | bytes 663560 | tf_op jit(solution)/shard_map/ppermute | solution.py:507
  109.9 23.5 %collective-permute-start.11 = (bf16[3,32,1152]{2,1,0:T(8,128)(2,1)S(1)}, bf16[3,32,1152]{2,1,0:T(8,128)(2,1)S(1)}, u32[]{:S(2)}, u32[]{:S(2)}) collective-permute-start(bf16[3,32,1152]{2,1,0:T(8,128)(2,1)S(1)} %get-tuple-element.67), channel_id=1, source_target_pairs={{0,5},{1,4},{2,7},{3,6},{4,1},{5,0},{6,3},{7,2},{8,13},{9,12},{10,... | collective-permute-start | bytes 663560 | tf_op jit(solution)/shard_map/ppermute | solution.py:507
  111.6 21.8 %copy-start.3 = (bf16[3,32,1152]{2,1,0:T(8,128)(2,1)}, bf16[3,32,1152]{2,1,0:T(8,128)(2,1)S(1)}, u32[]{:S(2)}) copy-start(bf16[3,32,1152]{2,1,0:T(8,128)(2,1)S(1)} %collective-permute-done.7.refs_4_) | copy-start | bytes 663556
  111.6 21.8 %collective-permute-start.12 = (bf16[3,32,1152]{2,1,0:T(8,128)(2,1)S(1)}, bf16[3,32,1152]{2,1,0:T(8,128)(2,1)S(1)}, u32[]{:S(2)}, u32[]{:S(2)}) collective-permute-start(bf16[3,32,1152]{2,1,0:T(8,128)(2,1)S(1)} %get-tuple-element.68), channel_id=1, source_target_pairs={{0,6},{1,7},{2,0},{3,1},{4,2},{5,3},{6,4},{7,5},{8,14},{9,15},{10,... | collective-permute-start | bytes 663560 | tf_op jit(solution)/shard_map/ppermute | solution.py:507
  119.1 14.2 %copy-start.4 = (bf16[3,32,1152]{2,1,0:T(8,128)(2,1)}, bf16[3,32,1152]{2,1,0:T(8,128)(2,1)S(1)}, u32[]{:S(2)}) copy-start(bf16[3,32,1152]{2,1,0:T(8,128)(2,1)S(1)} %collective-permute-done.8.refs_5_) | copy-start | bytes 663556
  119.1 14.2 %collective-permute-start.13 = (bf16[3,32,1152]{2,1,0:T(8,128)(2,1)S(1)}, bf16[3,32,1152]{2,1,0:T(8,128)(2,1)S(1)}, u32[]{:S(2)}, u32[]{:S(2)}) collective-permute-start(bf16[3,32,1152]{2,1,0:T(8,128)(2,1)S(1)} %get-tuple-element.69), channel_id=1, source_target_pairs={{0,7},{1,6},{2,1},{3,0},{4,3},{5,2},{6,5},{7,4},{8,15},{9,14},{10,... | collective-permute-start | bytes 663560 | tf_op jit(solution)/shard_map/ppermute | solution.py:507
  (9 other events, 38.5 us)

commit v4 on v3

--- a/solution.py
+++ b/solution.py
@@ -143,9 +143,8 @@
     parts = group_rows()
     weights = copy_all([(wt_hbm.at[part], wt.at[part]) for part in parts], wsem)
     out_weight = copy_all([(wo_hbm, wo)], osem)
-    start_all(weights[:3])
+    start_all(weights[:6])
     wait_all(copies)
-    start_all(weights[3:6])
     toks = x_ref.shape[0]
     frames = toks // 256
     per = HEADS // GROUPS
@@ -287,9 +286,8 @@
         for g in range(GROUPS)
     ]
     late = copy_all([(wt_hbm.at[part], wt.at[part]) for part in rows] + [(x_hbm, x_ref)], tsem)
-    start_all(load_wo)
+    start_all(load_wo + loads[0])
     wait_all(copies)
-    start_all(loads[0])
     for f in range(2):
         part = c_ref[pl.ds(f * 256, 256)]
         c_ref[pl.ds(f * 256, 256)] = jnp.where(keep_ref[f] > 0, part, jnp.zeros_like(part))

time: 140 us -> 141 us (level)
  transfers between devices with their start and end apart: 19 -> 19, of which waited for: 5 -> 5; matrix products, arithmetic and copies ran while one was open for 2% -> 2% of each run, Pallas kernels for 34% -> 35%
where the time goes in v4:
time: 141 us; the launch traced here: 140 us
  Pallas kernels  56.2 us (40%)
  starting transfers between devices  55.4 us (39%)
  waiting for transfers between devices  21.9 us (16%)
  local copies, waits for them, and re-layouts  5.15 us (4%)
    ppermute x14, starting transfers between devices, exchange(): out.append(lax.ppermute(x, 'sp', pairs))  23.1 us
    pallas_call x1, Pallas kernels, backward(): pl.pallas_call(functools.partial(backward_kernel, scale), out_shape=(out,...  21 us
    all_to_all x3, starting transfers between devices, spread(): lax.all_to_all(x.reshape(groups, -1, x.shape[-1]), 'grp', 0, 0, tiled=True)  18.7 us
    ppermute x14, waiting for transfers between devices, exchange(): out.append(lax.ppermute(x, 'sp', pairs))  18.7 us
    pallas_call x1, Pallas kernels, forward(): pl.pallas_call(functools.partial(forward_kernel, scale), out_shape=(out,...  16.6 us
    all_to_all x1, starting transfers between devices, on_device(): lax.all_to_all(out_b, ('grp', 'sp'), 0, 0, tiled=True).reshape(block)  9.73 us
    pallas_call x1, Pallas kernels, prepare(): pl.pallas_call(prepare_kernel, out_shape=(pltpu.HBM((3 * HEADS * HP, widt...  7.37 us
    pallas_call x2, Pallas kernels, pack(): pl.pallas_call(functools.partial(pack_kernel, leads, whole), out_shape=sh...  5.26 us
  transfers between devices with their start and end apart: 19, of which 5 were waited for; matrix products, arithmetic and copies ran while one was open for 2% of the time, Pallas kernels for 35%

profile of v4, /device:TPU:1, one launch (start us, length us, event | category | flops | bytes accessed | tf_op | source)
XLA Modules:
  0.0 139.9 jit_solution(5200969842331546413)
XLA Ops:
  0.7 3.1 %pack.2 = (bf16[3,32,1152]{2,1,0:T(8,128)(2,1)S(1)}, bf16[3,32,1152]{2,1,0:T(8,128)(2,1)S(1)}, bf16[3,32,1152]{2,1,0:T(8,128)(2,1)S(1)}, bf16[3,32,1152]{2,1,0:T...) custom-call(s32[8]{0:T(128)S(1)} %fusion.3.to_ref, ...), custom_call_target="tpu_custom_call" | custom-call | tf_op jit(solution)/shard_map/pack/pallas_call | solution.py:445
  3.8 7.7 %all-to-all-start = ((bf16[16,16,1152]{2,1,0:T(8,128)(2,1)}), bf16[16,16,1152]{2,1,0:T(8,128)(2,1)S(1)}, u32[]{:S(2)}, u32[]{:S(2)}) async-start(bf16[16,16,1152]{2,1,0:T(8,128)(2,1)} %bitcast), calls=%async_computation | async-start | bytes 1179648 | tf_op jit(solution)/shard_map/all_to_all | solution.py:418
  12.6 1.7 %collective-permute-start.1 = (bf16[3,32,1152]{2,1,0:T(8,128)(2,1)S(1)}, bf16[3,32,1152]{2,1,0:T(8,128)(2,1)}, u32[]{:S(2)}, u32[]{:S(2)}) collective-permute-start(bf16[3,32,1152]{2,1,0:T(8,128)(2,1)S(1)} %get-tuple-element.45), channel_id=1, source_target_pairs={{0,2},{1,3},{2,4},{3,5},{4,6},{5,7},{6,0},{7,1},{8,10},{9,11},{10,... | collective-permute-start | bytes 663560 | tf_op jit(solution)/shard_map/ppermute | solution.py:505
  14.2 1.9 %collective-permute-start.2 = (bf16[3,32,1152]{2,1,0:T(8,128)(2,1)S(1)}, bf16[3,32,1152]{2,1,0:T(8,128)(2,1)}, u32[]{:S(2)}, u32[]{:S(2)}) collective-permute-start(bf16[3,32,1152]{2,1,0:T(8,128)(2,1)S(1)} %get-tuple-element.46), channel_id=1, source_target_pairs={{0,3},{1,2},{2,5},{3,4},{4,7},{5,6},{6,1},{7,0},{8,11},{9,10},{10,... | collective-permute-start | bytes 663560 | tf_op jit(solution)/shard_map/ppermute | solution.py:505
  17.6 1.8 %collective-permute-start.4 = (bf16[3,32,1152]{2,1,0:T(8,128)(2,1)S(1)}, bf16[3,32,1152]{2,1,0:T(8,128)(2,1)}, u32[]{:S(2)}, u32[]{:S(2)}) collective-permute-start(bf16[3,32,1152]{2,1,0:T(8,128)(2,1)S(1)} %get-tuple-element.48), channel_id=1, source_target_pairs={{0,5},{1,4},{2,7},{3,6},{4,1},{5,0},{6,3},{7,2},{8,13},{9,12},{10,... | collective-permute-start | bytes 663560 | tf_op jit(solution)/shard_map/ppermute | solution.py:505
  19.4 3.2 %all-to-all-done.x_ref = bf16[16,16,1152]{2,1,0:T(8,128)(2,1)S(1)} async-done(((bf16[16,16,1152]{2,1,0:T(8,128)(2,1)}), bf16[16,16,1152]{2,1,0:T(8,128)(2,1)S(1)}, u32[]{:S(2)}, u32[]{:S(2)}) %all-to-all-start) | async-done | bytes 589856 | tf_op jit(solution)/shard_map/all_to_all | solution.py:418
  24.0 4.3 %all-to-all-start.1 = ((bf16[16,16,1152]{2,1,0:T(8,128)(2,1)}), bf16[16,16,1152]{2,1,0:T(8,128)(2,1)}, u32[]{:S(2)}, u32[]{:S(2)}) async-start(bf16[16,16,1152]{2,1,0:T(8,128)(2,1)} %shuffle.2), calls=%async_computation.1 | async-start | bytes 1179648 | tf_op jit(solution)/shard_map/all_to_all | solution.py:418
  29.2 3.8 %collective-permute-start.5 = (bf16[3,32,1152]{2,1,0:T(8,128)(2,1)S(1)}, bf16[3,32,1152]{2,1,0:T(8,128)(2,1)S(1)}, u32[]{:S(2)}, u32[]{:S(2)}) collective-permute-start(bf16[3,32,1152]{2,1,0:T(8,128)(2,1)S(1)} %get-tuple-element.49), channel_id=1, source_target_pairs={{0,6},{1,7},{2,0},{3,1},{4,2},{5,3},{6,4},{7,5},{8,14},{9,15},{10,... | collective-permute-start | bytes 663560 | tf_op jit(solution)/shard_map/ppermute | solution.py:505
  33.0 2.4 %collective-permute-start.6 = (bf16[3,32,1152]{2,1,0:T(8,128)(2,1)S(1)}, bf16[3,32,1152]{2,1,0:T(8,128)(2,1)S(1)}, u32[]{:S(2)}, u32[]{:S(2)}) collective-permute-start(bf16[3,32,1152]{2,1,0:T(8,128)(2,1)S(1)} %get-tuple-element.50), channel_id=1, source_target_pairs={{0,7},{1,6},{2,1},{3,0},{4,3},{5,2},{6,5},{7,4},{8,15},{9,14},{10,... | collective-permute-start | bytes 663560 | tf_op jit(solution)/shard_map/ppermute | solution.py:505
  35.6 7.4 %prepare.1 = (bf16[3840,1152]{1,0:T(8,128)(2,1)}, bf16[1280,1152]{1,0:T(8,128)(2,1)}) custom-call(bf16[1152,3456]{1,0:T(8,128)(2,1)} %wq_hbm, bf16[1152,1152]{1,0:T(8,128)(2,1)} %wo_hbm.1), custom_call_target="tpu_custom_call" | custom-call | tf_op jit(solution)/shard_map/prepare/pallas_call | solution.py:88
  43.0 3.8 %all-to-all-start.2 = ((bf16[8,32,1152]{2,1,0:T(8,128)(2,1)}), bf16[8,32,1152]{2,1,0:T(8,128)(2,1)S(1)}, u32[]{:S(2)}, u32[]{:S(2)}) async-start(bf16[8,32,1152]{2,1,0:T(8,128)(2,1)} %bitcast.1), calls=%async_computation.2 | async-start | bytes 1179648 | tf_op jit(solution)/shard_map/all_to_all | solution.py:535
  47.6 16.6 %forward.1 = (bf16[256,1152]{1,0:T(8,128)(2,1)}, bf16[256,1152]{1,0:T(8,128)(2,1)}, bf16[512,1152]{1,0:T(8,128)(2,1)}, bf16[3840,512]{1,0:T(8,128)(2,1)}, bf16[1...) custom-call(s32[8]{0:T(128)S(1)} %fusion.1.from_ref, s32[2]{0:T(128)S(1)} %compare_convert_fusion.keep_ref, ...), custom_call_target="tpu_custom_call" | custom-call | flops 6710886400 | bytes 11796480 | tf_op jit(solution)/shard_map/forward/pallas_call | solution.py:240
  64.3 6.7 %all-to-all-start.3 = ((bf16[16,16,1152]{2,1,0:T(8,128)(2,1)}), bf16[16,16,1152]{2,1,0:T(8,128)(2,1)S(1)}, u32[]{:S(2)}, u32[]{:S(2)}) async-start(bf16[16,16,1152]{2,1,0:T(8,128)(2,1)} %bitcast.14), calls=%async_computation.3 | async-start | bytes 1179648 | tf_op jit(solution)/shard_map/all_to_all | solution.py:418
  71.0 21.0 %backward.1 = (bf16[256,1152]{1,0:T(8,128)(2,1)}, bf16[256,1152]{1,0:T(8,128)(2,1)}) custom-call(s32[8]{0:T(128)S(1)} %fusion.1.from_ref, s32[2]{0:T(128)S(1)} %compare_convert_fusion.keep_ref, f32[16,1,512]{2,1,0:T(1,128)S(1)} %get-tuple-element.53.inverse, bf16[3840,1152]{1,0:T(8,128)(2,1)} %get-tuple-element.42.wt_hbm, ...), custom_call_target="tpu_custom_call" | custom-call | flops 7381975040 | bytes 11796480 | tf_op jit(solution)/shard_map/backward/pallas_call | solution.py:371
  93.7 9.7 %all-to-all-start.4 = ((bf16[128,2,1152]{2,1,0:T(2,128)(2,1)}), bf16[128,2,1152]{2,1,0:T(2,128)(2,1)S(1)}, u32[]{:S(2)}, u32[]{:S(2)}) async-start(bf16[128,2,1152]{2,1,0:T(2,128)(2,1)} %reshape.35), calls=%async_computation.4 | async-start | bytes 1179648 | tf_op jit(solution)/shard_map/all_to_all | solution.py:542
  103.4 2.2 %pack.3 = (bf16[3,32,1152]{2,1,0:T(8,128)(2,1)S(1)}, bf16[3,32,1152]{2,1,0:T(8,128)(2,1)S(1)}, bf16[3,32,1152]{2,1,0:T(8,128)(2,1)S(1)}, bf16[3,32,1152]{2,1,0:T...) custom-call(s32[8]{0:T(128)S(1)} %fusion.3.to_ref, ...), custom_call_target="tpu_custom_call" | custom-call | tf_op jit(solution)/shard_map/pack/pallas_call | solution.py:445
  107.6 1.8 %collective-permute-start.9 = (bf16[3,32,1152]{2,1,0:T(8,128)(2,1)S(1)}, bf16[3,32,1152]{2,1,0:T(8,128)(2,1)S(1)}, u32[]{:S(2)}, u32[]{:S(2)}) collective-permute-start(bf16[3,32,1152]{2,1,0:T(8,128)(2,1)S(1)} %get-tuple-element.65), channel_id=1, source_target_pairs={{0,3},{1,2},{2,5},{3,4},{4,7},{5,6},{6,1},{7,0},{8,11},{9,10},{10,... | collective-permute-start | bytes 663560 | tf_op jit(solution)/shard_map/ppermute | solution.py:505
  109.3 1.5 %collective-permute-start.10 = (bf16[3,32,1152]{2,1,0:T(8,128)(2,1)S(1)}, bf16[3,32,1152]{2,1,0:T(8,128)(2,1)S(1)}, u32[]{:S(2)}, u32[]{:S(2)}) collective-permute-start(bf16[3,32,1152]{2,1,0:T(8,128)(2,1)S(1)} %get-tuple-element.66), channel_id=1, source_target_pairs={{0,4},{1,5},{2,6},{3,7},{4,0},{5,1},{6,2},{7,3},{8,12},{9,13},{10,... | collective-permute-start | bytes 663560 | tf_op jit(solution)/shard_map/ppermute | solution.py:505
  110.9 1.7 %collective-permute-start.11 = (bf16[3,32,1152]{2,1,0:T(8,128)(2,1)S(1)}, bf16[3,32,1152]{2,1,0:T(8,128)(2,1)S(1)}, u32[]{:S(2)}, u32[]{:S(2)}) collective-permute-start(bf16[3,32,1152]{2,1,0:T(8,128)(2,1)S(1)} %get-tuple-element.67), channel_id=1, source_target_pairs={{0,5},{1,4},{2,7},{3,6},{4,1},{5,0},{6,3},{7,2},{8,13},{9,12},{10,... | collective-permute-start | bytes 663560 | tf_op jit(solution)/shard_map/ppermute | solution.py:505
  113.8 6.3 %collective-permute-done.8.refs_5_ = bf16[3,32,1152]{2,1,0:T(8,128)(2,1)S(1)} collective-permute-done((bf16[3,32,1152]{2,1,0:T(8,128)(2,1)S(1)}, bf16[3,32,1152]{2,1,0:T(8,128)(2,1)S(1)}, u32[]{:S(2)}, u32[]{:S(2)}) %collective-permute-start.8) | collective-permute-done | bytes 221216 | tf_op jit(solution)/shard_map/ppermute | solution.py:505
  122.0 2.8 %collective-permute-done.9.refs_6_ = bf16[3,32,1152]{2,1,0:T(8,128)(2,1)S(1)} collective-permute-done((bf16[3,32,1152]{2,1,0:T(8,128)(2,1)S(1)}, bf16[3,32,1152]{2,1,0:T(8,128)(2,1)S(1)}, u32[]{:S(2)}, u32[]{:S(2)}) %collective-permute-start.9) | collective-permute-done | bytes 221216 | tf_op jit(solution)/shard_map/ppermute | solution.py:505
  124.8 4.7 %collective-permute-done.10.refs_7_ = bf16[3,32,1152]{2,1,0:T(8,128)(2,1)S(1)} collective-permute-done((bf16[3,32,1152]{2,1,0:T(8,128)(2,1)S(1)}, bf16[3,32,1152]{2,1,0:T(8,128)(2,1)S(1)}, u32[]{:S(2)}, u32[]{:S(2)}) %collective-permute-start.10) | collective-permute-done | bytes 221216 | tf_op jit(solution)/shard_map/ppermute | solution.py:505
  129.6 4.7 %collective-permute-done.11.refs_8_ = bf16[3,32,1152]{2,1,0:T(8,128)(2,1)S(1)} collective-permute-done((bf16[3,32,1152]{2,1,0:T(8,128)(2,1)S(1)}, bf16[3,32,1152]{2,1,0:T(8,128)(2,1)S(1)}, u32[]{:S(2)}, u32[]{:S(2)}) %collective-permute-start.11) | collective-permute-done | bytes 221216 | tf_op jit(solution)/shard_map/ppermute | solution.py:505
  135.8 4.0 %unpack.1 = (bf16[2,8,32,1152]{3,2,1,0:T(8,128)(2,1)}, bf16[2,8,32,1152]{3,2,1,0:T(8,128)(2,1)}) custom-call(s32[8]{0:T(128)S(1)} %fusion.1.from_ref, bf16[8,32,1152]{2,1,0:T(8,128)(2,1)} %bitcast.11, bf16[8,32,1152]{2,1,0:T(8,128)(2,1)} %bitcast.13, bf16[8,32,1152]{2,1,0:T(8,128)(2,1)} %bitcast.9, bf16[8,32,1152]{2,1,0:T(8,128)(2,1)} %reshape.36.refs_3_, ...), custom_call_target="tpu_custom_call" | custom-call | tf_op jit(solution)/shard_map/unpack/pallas_call | solution.py:485
  (57 shorter events, 13.9 us)
Async XLA Ops:
  0.6 22.0 %copy-start = (s32[16]{0:T(128)S(1)}, s32[16]{0:T(128)}, u32[]{:S(2)}) copy-start(s32[16]{0:T(128)} %index_ref.1) | copy-start | bytes 196
  3.8 24.5 %copy-start.1 = (bf16[2,8,32,1152]{3,2,1,0:T(8,128)(2,1)S(1)}, bf16[2,8,32,1152]{3,2,1,0:T(8,128)(2,1)}, u32[]{:S(2)}) copy-start(bf16[2,8,32,1152]{3,2,1,0:T(8,128)(2,1)} %refs_2_.1) | copy-start | bytes 3538948
  3.8 31.6 %copy-start.10 = (s32[32]{0:T(128)S(1)}, s32[32]{0:T(128)}, u32[]{:S(2)}) copy-start(s32[32]{0:T(128)} %param.7) | copy-start | bytes 388
  3.8 18.8 %all-to-all-start = ((bf16[16,16,1152]{2,1,0:T(8,128)(2,1)}), bf16[16,16,1152]{2,1,0:T(8,128)(2,1)S(1)}, u32[]{:S(2)}, u32[]{:S(2)}) async-start(bf16[16,16,1152]{2,1,0:T(8,128)(2,1)} %bitcast), calls=%async_computation | async-start | bytes 1179648 | tf_op jit(solution)/shard_map/all_to_all | solution.py:418
  11.5 17.6 %collective-permute-start = (bf16[3,32,1152]{2,1,0:T(8,128)(2,1)S(1)}, bf16[3,32,1152]{2,1,0:T(8,128)(2,1)S(1)}, u32[]{:S(2)}, u32[]{:S(2)}) collective-permute-start(bf16[3,32,1152]{2,1,0:T(8,128)(2,1)S(1)} %get-tuple-element.44), channel_id=1, source_target_pairs={{0,1},{1,0},{2,3},{3,2},{4,5},{5,4},{6,7},{7,6},{8,9},{9,8},{10,11... | collective-permute-start | bytes 663560 | tf_op jit(solution)/shard_map/ppermute | solution.py:505
  12.6 20.4 %collective-permute-start.1 = (bf16[3,32,1152]{2,1,0:T(8,128)(2,1)S(1)}, bf16[3,32,1152]{2,1,0:T(8,128)(2,1)}, u32[]{:S(2)}, u32[]{:S(2)}) collective-permute-start(bf16[3,32,1152]{2,1,0:T(8,128)(2,1)S(1)} %get-tuple-element.45), channel_id=1, source_target_pairs={{0,2},{1,3},{2,4},{3,5},{4,6},{5,7},{6,0},{7,1},{8,10},{9,11},{10,... | collective-permute-start | bytes 663560 | tf_op jit(solution)/shard_map/ppermute | solution.py:505
  14.2 32.6 %collective-permute-start.2 = (bf16[3,32,1152]{2,1,0:T(8,128)(2,1)S(1)}, bf16[3,32,1152]{2,1,0:T(8,128)(2,1)}, u32[]{:S(2)}, u32[]{:S(2)}) collective-permute-start(bf16[3,32,1152]{2,1,0:T(8,128)(2,1)S(1)} %get-tuple-element.46), channel_id=1, source_target_pairs={{0,3},{1,2},{2,5},{3,4},{4,7},{5,6},{6,1},{7,0},{8,11},{9,10},{10,... | collective-permute-start | bytes 663560 | tf_op jit(solution)/shard_map/ppermute | solution.py:505
  16.1 30.7 %collective-permute-start.3 = (bf16[3,32,1152]{2,1,0:T(8,128)(2,1)S(1)}, bf16[3,32,1152]{2,1,0:T(8,128)(2,1)}, u32[]{:S(2)}, u32[]{:S(2)}) collective-permute-start(bf16[3,32,1152]{2,1,0:T(8,128)(2,1)S(1)} %get-tuple-element.47), channel_id=1, source_target_pairs={{0,4},{1,5},{2,6},{3,7},{4,0},{5,1},{6,2},{7,3},{8,12},{9,13},{10,... | collective-permute-start | bytes 663560 | tf_op jit(solution)/shard_map/ppermute | solution.py:505
  17.6 29.3 %collective-permute-start.4 = (bf16[3,32,1152]{2,1,0:T(8,128)(2,1)S(1)}, bf16[3,32,1152]{2,1,0:T(8,128)(2,1)}, u32[]{:S(2)}, u32[]{:S(2)}) collective-permute-start(bf16[3,32,1152]{2,1,0:T(8,128)(2,1)S(1)} %get-tuple-element.48), channel_id=1, source_target_pairs={{0,5},{1,4},{2,7},{3,6},{4,1},{5,0},{6,3},{7,2},{8,13},{9,12},{10,... | collective-permute-start | bytes 663560 | tf_op jit(solution)/shard_map/ppermute | solution.py:505
  24.0 19.0 %all-to-all-start.1 = ((bf16[16,16,1152]{2,1,0:T(8,128)(2,1)}), bf16[16,16,1152]{2,1,0:T(8,128)(2,1)}, u32[]{:S(2)}, u32[]{:S(2)}) async-start(bf16[16,16,1152]{2,1,0:T(8,128)(2,1)} %shuffle.2), calls=%async_computation.1 | async-start | bytes 1179648 | tf_op jit(solution)/shard_map/all_to_all | solution.py:418
  29.2 17.7 %collective-permute-start.5 = (bf16[3,32,1152]{2,1,0:T(8,128)(2,1)S(1)}, bf16[3,32,1152]{2,1,0:T(8,128)(2,1)S(1)}, u32[]{:S(2)}, u32[]{:S(2)}) collective-permute-start(bf16[3,32,1152]{2,1,0:T(8,128)(2,1)S(1)} %get-tuple-element.49), channel_id=1, source_target_pairs={{0,6},{1,7},{2,0},{3,1},{4,2},{5,3},{6,4},{7,5},{8,14},{9,15},{10,... | collective-permute-start | bytes 663560 | tf_op jit(solution)/shard_map/ppermute | solution.py:505
  33.0 13.9 %collective-permute-start.6 = (bf16[3,32,1152]{2,1,0:T(8,128)(2,1)S(1)}, bf16[3,32,1152]{2,1,0:T(8,128)(2,1)S(1)}, u32[]{:S(2)}, u32[]{:S(2)}) collective-permute-start(bf16[3,32,1152]{2,1,0:T(8,128)(2,1)S(1)} %get-tuple-element.50), channel_id=1, source_target_pairs={{0,7},{1,6},{2,1},{3,0},{4,3},{5,2},{6,5},{7,4},{8,15},{9,14},{10,... | collective-permute-start | bytes 663560 | tf_op jit(solution)/shard_map/ppermute | solution.py:505
  43.0 21.2 %all-to-all-start.2 = ((bf16[8,32,1152]{2,1,0:T(8,128)(2,1)}), bf16[8,32,1152]{2,1,0:T(8,128)(2,1)S(1)}, u32[]{:S(2)}, u32[]{:S(2)}) async-start(bf16[8,32,1152]{2,1,0:T(8,128)(2,1)} %bitcast.1), calls=%async_computation.2 | async-start | bytes 1179648 | tf_op jit(solution)/shard_map/all_to_all | solution.py:535
  64.3 27.8 %all-to-all-start.3 = ((bf16[16,16,1152]{2,1,0:T(8,128)(2,1)}), bf16[16,16,1152]{2,1,0:T(8,128)(2,1)S(1)}, u32[]{:S(2)}, u32[]{:S(2)}) async-start(bf16[16,16,1152]{2,1,0:T(8,128)(2,1)} %bitcast.14), calls=%async_computation.3 | async-start | bytes 1179648 | tf_op jit(solution)/shard_map/all_to_all | solution.py:418
  93.7 27.3 %all-to-all-start.4 = ((bf16[128,2,1152]{2,1,0:T(2,128)(2,1)}), bf16[128,2,1152]{2,1,0:T(2,128)(2,1)S(1)}, u32[]{:S(2)}, u32[]{:S(2)}) async-start(bf16[128,2,1152]{2,1,0:T(2,128)(2,1)} %reshape.35), calls=%async_computation.4 | async-start | bytes 1179648 | tf_op jit(solution)/shard_map/all_to_all | solution.py:542
  105.6 6.9 %collective-permute-start.7 = (bf16[3,32,1152]{2,1,0:T(8,128)(2,1)S(1)}, bf16[3,32,1152]{2,1,0:T(8,128)(2,1)S(1)}, u32[]{:S(2)}, u32[]{:S(2)}) collective-permute-start(bf16[3,32,1152]{2,1,0:T(8,128)(2,1)S(1)} %get-tuple-element.63), channel_id=1, source_target_pairs={{0,1},{1,0},{2,3},{3,2},{4,5},{5,4},{6,7},{7,6},{8,9},{9,8},{10,11... | collective-permute-start | bytes 663560 | tf_op jit(solution)/shard_map/ppermute | solution.py:505
  106.8 13.3 %collective-permute-start.8 = (bf16[3,32,1152]{2,1,0:T(8,128)(2,1)S(1)}, bf16[3,32,1152]{2,1,0:T(8,128)(2,1)S(1)}, u32[]{:S(2)}, u32[]{:S(2)}) collective-permute-start(bf16[3,32,1152]{2,1,0:T(8,128)(2,1)S(1)} %get-tuple-element.64), channel_id=1, source_target_pairs={{0,2},{1,3},{2,4},{3,5},{4,6},{5,7},{6,0},{7,1},{8,10},{9,11},{10,... | collective-permute-start | bytes 663560 | tf_op jit(solution)/shard_map/ppermute | solution.py:505
  107.6 17.3 %collective-permute-start.9 = (bf16[3,32,1152]{2,1,0:T(8,128)(2,1)S(1)}, bf16[3,32,1152]{2,1,0:T(8,128)(2,1)S(1)}, u32[]{:S(2)}, u32[]{:S(2)}) collective-permute-start(bf16[3,32,1152]{2,1,0:T(8,128)(2,1)S(1)} %get-tuple-element.65), channel_id=1, source_target_pairs={{0,3},{1,2},{2,5},{3,4},{4,7},{5,6},{6,1},{7,0},{8,11},{9,10},{10,... | collective-permute-start | bytes 663560 | tf_op jit(solution)/shard_map/ppermute | solution.py:505
  109.3 20.2 %collective-permute-start.10 = (bf16[3,32,1152]{2,1,0:T(8,128)(2,1)S(1)}, bf16[3,32,1152]{2,1,0:T(8,128)(2,1)S(1)}, u32[]{:S(2)}, u32[]{:S(2)}) collective-permute-start(bf16[3,32,1152]{2,1,0:T(8,128)(2,1)S(1)} %get-tuple-element.66), channel_id=1, source_target_pairs={{0,4},{1,5},{2,6},{3,7},{4,0},{5,1},{6,2},{7,3},{8,12},{9,13},{10,... | collective-permute-start | bytes 663560 | tf_op jit(solution)/shard_map/ppermute | solution.py:505
  110.9 23.5 %collective-permute-start.11 = (bf16[3,32,1152]{2,1,0:T(8,128)(2,1)S(1)}, bf16[3,32,1152]{2,1,0:T(8,128)(2,1)S(1)}, u32[]{:S(2)}, u32[]{:S(2)}) collective-permute-start(bf16[3,32,1152]{2,1,0:T(8,128)(2,1)S(1)} %get-tuple-element.67), channel_id=1, source_target_pairs={{0,5},{1,4},{2,7},{3,6},{4,1},{5,0},{6,3},{7,2},{8,13},{9,12},{10,... | collective-permute-start | bytes 663560 | tf_op jit(solution)/shard_map/ppermute | solution.py:505
  112.6 21.8 %copy-start.3 = (bf16[3,32,1152]{2,1,0:T(8,128)(2,1)}, bf16[3,32,1152]{2,1,0:T(8,128)(2,1)S(1)}, u32[]{:S(2)}) copy-start(bf16[3,32,1152]{2,1,0:T(8,128)(2,1)S(1)} %collective-permute-done.7.refs_4_) | copy-start | bytes 663556
  112.6 21.8 %collective-permute-start.12 = (bf16[3,32,1152]{2,1,0:T(8,128)(2,1)S(1)}, bf16[3,32,1152]{2,1,0:T(8,128)(2,1)S(1)}, u32[]{:S(2)}, u32[]{:S(2)}) collective-permute-start(bf16[3,32,1152]{2,1,0:T(8,128)(2,1)S(1)} %get-tuple-element.68), channel_id=1, source_target_pairs={{0,6},{1,7},{2,0},{3,1},{4,2},{5,3},{6,4},{7,5},{8,14},{9,15},{10,... | collective-permute-start | bytes 663560 | tf_op jit(solution)/shard_map/ppermute | solution.py:505
  120.1 14.2 %copy-start.4 = (bf16[3,32,1152]{2,1,0:T(8,128)(2,1)}, bf16[3,32,1152]{2,1,0:T(8,128)(2,1)S(1)}, u32[]{:S(2)}) copy-start(bf16[3,32,1152]{2,1,0:T(8,128)(2,1)S(1)} %collective-permute-done.8.refs_5_) | copy-start | bytes 663556
  120.1 14.2 %collective-permute-start.13 = (bf16[3,32,1152]{2,1,0:T(8,128)(2,1)S(1)}, bf16[3,32,1152]{2,1,0:T(8,128)(2,1)S(1)}, u32[]{:S(2)}, u32[]{:S(2)}) collective-permute-start(bf16[3,32,1152]{2,1,0:T(8,128)(2,1)S(1)} %get-tuple-element.69), channel_id=1, source_target_pairs={{0,7},{1,6},{2,1},{3,0},{4,3},{5,2},{6,5},{7,4},{8,15},{9,14},{10,... | collective-permute-start | bytes 663560 | tf_op jit(solution)/shard_map/ppermute | solution.py:505
  (9 other events, 38.5 us)
